TPU v7x, 32 devices: a whole 2x2x4 slice. The times are simulated.
32 devices in a mesh: dp: 4 (over z), fsdp: 8 (over y, x, core).
Axes of the slice: x: 2, y: 2, z: 4, core: 2. Of those that a mesh axis runs over, the one named last changes fastest.
Arguments:
- global_tokens: bfloat16 [96, 14, 14, 512], P(('dp', 'fsdp')), may hold values from -6 to 6
- local_tokens: bfloat16 [288, 7, 7, 512], P(('dp', 'fsdp')), may hold values from -6 to 6
- crop_extent: int32 [288, 2], P(('dp', 'fsdp')), may hold values from 4 to 7
- conv_weight: bfloat16 [2, 9, 512], P(None, None, 'fsdp'), may hold values from -2 to 2
- vectors: bfloat16 [2, 7, 512], P(None, None, 'fsdp'), may hold values from -1 to 1
- gains: bfloat16 [2, 2, 512], P(None, None, 'fsdp'), may hold values from 0.5 to 1.5
- qkv_weight: bfloat16 [2, 512, 1536], P(None, 'fsdp'), may hold values from -0.25 to 0.25
- proj_weight: bfloat16 [2, 512, 512], P(None, 'fsdp'), may hold values from -0.625 to 0.625
- fc1_weight: bfloat16 [2, 512, 2048], P(None, 'fsdp'), may hold values from -0.25 to 0.25
- fc1_bias: bfloat16 [2, 2048], P(None, 'fsdp'), may hold values from -1 to 1
- fc2_weight: bfloat16 [2, 2048, 512], P(None, 'fsdp'), may hold values from -0.125 to 0.125
- global_cotangent: bfloat16 [96, 14, 14, 512], P(('dp', 'fsdp')), may hold values from -6 to 6
- local_cotangent: bfloat16 [288, 7, 7, 512], P(('dp', 'fsdp')), may hold values from -6 to 6
Outputs:
- global_out: bfloat16 [96, 14, 14, 512], P(('dp', 'fsdp'))
- local_out: bfloat16 [288, 7, 7, 512], P(('dp', 'fsdp'))
- global_grad: float32 [96, 14, 14, 512], P(('dp', 'fsdp'))
- local_grad: float32 [288, 7, 7, 512], P(('dp', 'fsdp'))
- conv_grad: float32 [2, 9, 512], P(None, None, 'fsdp')
- vectors_grad: float32 [2, 7, 512], P(None, None, 'fsdp')
- gains_grad: float32 [2, 2, 512], P(None, None, 'fsdp')
- qkv_grad: float32 [2, 512, 1536], P(None, 'fsdp')
- proj_grad: float32 [2, 512, 512], P(None, 'fsdp')
- fc1_grad: float32 [2, 512, 2048], P(None, 'fsdp')
- fc1_bias_grad: float32 [2, 2048], P(None, 'fsdp')
- fc2_grad: float32 [2, 2048, 512], P(None, 'fsdp')
Inputs may be any that keep to these rules, and one draw needn't show every extreme that they name: `crop_extent`: for each local crop, the rows and the columns of its 7 x 7 canvas that hold patches, counted from the canvas's first row and column.
All inputs are finite; a program needn't handle non-finite values.
Results may differ from a plain program's by a relative error of at most 0.025.
Values may be sent and summed in bfloat16 or wider, within the bound.
No kernel may reach another device: no remote copies, remote signals or barrier semaphores. Data moves between devices by JAX's collectives and lax.ppermute only.
A program may use at most 256 MiB of HBM per device.

v0:
```python
import jax
import jax.numpy as jnp
from jax import lax
from jax.sharding import PartitionSpec as P

HEAD_DIM = 32
WIN = 7
SIDE = 14


EPSILON = 1e-05
LINEAR_FORMS = ("...k,kd->...d", "...d,kd->...k", "...k,...d->kd")
WINDOW_SCORE = ("wqhd,wkhd->whqk", "whqk,wkhd->wqhd", "wqhd,whqk->wkhd")
WINDOW_MIX = ("whqk,wkhd->wqhd", "wqhd,wkhd->whqk", "whqk,wqhd->wkhd")
CHANNEL_SCORE = ("bngi,bngj->bgij", "bgij,bngj->bngi", "bngi,bgij->bngj")
CHANNEL_MIX = ("bgij,bngj->bngi", "bngi,bngj->bgij", "bgij,bngi->bngj")


def round_value(v):
    return lax.optimization_barrier(v.astype(jnp.bfloat16)).astype(jnp.float32)


def round_keep(v):
    return (round_value(v), None)


def round_pass(kept, grad):
    return (grad,)


def low(v):
    rounding = jax.custom_vjp(round_value)
    rounding.defvjp(round_keep, round_pass)
    return rounding(v)


def same_value(v):
    return v


def same_keep(v):
    return (v, None)


def same_round(kept, grad):
    return (round_value(grad),)


def low_back(v):
    passing = jax.custom_vjp(same_value)
    passing.defvjp(same_keep, same_round)
    return passing(v)


def contract(forms, first_operand, second_operand):

    def product_value(first, second):
        return jnp.einsum(
            forms[0],
            first.astype(jnp.bfloat16),
            second.astype(jnp.bfloat16),
            preferred_element_type=jnp.float32,
        )

    def product_keep(first, second):
        return (product_value(first, second), (first, second))

    def product_back(kept, grad):
        first, second = kept
        grad_low = grad.astype(jnp.bfloat16)
        first_grad = jnp.einsum(
            forms[1], grad_low, second.astype(jnp.bfloat16), preferred_element_type=jnp.float32
        )
        second_grad = jnp.einsum(
            forms[2], first.astype(jnp.bfloat16), grad_low, preferred_element_type=jnp.float32
        )
        return (first_grad, second_grad)

    product = jax.custom_vjp(product_value)
    product.defvjp(product_keep, product_back)
    return product(first_operand, second_operand)


def layer_norm(values, gain, shift):
    center = jnp.mean(values, axis=-1, keepdims=True)
    centred = values - center
    variance = jnp.mean(centred * centred, axis=-1, keepdims=True)
    return centred * lax.rsqrt(variance + EPSILON) * gain + shift


def softmax_rows(scores):
    shifted = scores - jnp.max(scores, axis=-1, keepdims=True)
    exponent = jnp.exp(shifted)
    return exponent / jnp.sum(exponent, axis=-1, keepdims=True)


def linear(inputs, weight):
    return low_back(contract(LINEAR_FORMS, inputs, weight))


def position_conv(values, mask, kernel, shift):
    extent = values.shape[1]
    padded = jnp.pad(values, ((0, 0), (1, 1), (1, 1), (0, 0)))
    total = values + shift
    for index in range(9):
        row_start = index // 3
        col_start = index % 3
        total = (
            total
            + kernel[index]
            * padded[:, row_start : row_start + extent, col_start : col_start + extent, :]
        )
    return total * mask[..., None]


def to_windows(values):
    count, extent = (values.shape[0], values.shape[1])
    parts = extent // WIN
    shaped = values.reshape(count, parts, WIN, parts, WIN, -1)
    return shaped.transpose(0, 1, 3, 2, 4, 5).reshape(count * parts * parts, WIN * WIN, -1)


def from_windows(values, count, extent):
    parts = extent // WIN
    shaped = values.reshape(count, parts, parts, WIN, WIN, -1)
    return shaped.transpose(0, 1, 3, 2, 4, 5).reshape(count, extent, extent, -1)


def spatial_mix(query, key, value, mask):
    count, extent, width = (query.shape[0], query.shape[1], query.shape[3])
    heads = width // HEAD_DIM
    wq = to_windows(query).reshape(-1, WIN * WIN, heads, HEAD_DIM)
    wk = to_windows(key).reshape(-1, WIN * WIN, heads, HEAD_DIM)
    wv = to_windows(value).reshape(-1, WIN * WIN, heads, HEAD_DIM)
    valid = to_windows(mask[..., None])[:, :, 0]
    scores = low_back(contract(WINDOW_SCORE, wq, wk)) * HEAD_DIM ** (-0.5)
    scores = jnp.where(valid[:, None, None, :] > 0.5, scores, -1000000000.0)
    weights = low(softmax_rows(scores))
    mixed = low_back(contract(WINDOW_MIX, weights, wv))
    return from_windows(mixed.reshape(-1, WIN * WIN, width), count, extent)


def channel_mix(query, key, value, mask):
    count, width = (query.shape[0], query.shape[3])
    groups = width // HEAD_DIM
    valid = mask.reshape(count, -1, 1, 1)
    gq = query.reshape(count, -1, groups, HEAD_DIM)
    gk = key.reshape(count, -1, groups, HEAD_DIM) * valid
    gv = value.reshape(count, -1, groups, HEAD_DIM)
    scores = low_back(contract(CHANNEL_SCORE, gk, gv)) * HEAD_DIM ** (-0.5)
    weights = low(softmax_rows(scores))
    mixed = low_back(contract(CHANNEL_MIX, weights, gq))
    return mixed.reshape(query.shape)


def block(values, mask, params, mixer):
    kernel, shifts, norm_gains, qkv_w, proj_w, up_w, up_b, down_w = params
    width = values.shape[-1]
    conv = position_conv(values, mask, kernel, shifts[0])
    normed = low(layer_norm(conv, norm_gains[0], shifts[1]))
    joined = linear(normed, qkv_w)
    query = low(joined[..., :width] + shifts[2])
    key = low(joined[..., width : 2 * width])
    value = low(joined[..., 2 * width :] + shifts[3])
    mixed = low(mixer(query, key, value, mask))
    resid = conv + linear(mixed, proj_w) + shifts[4]
    normed_two = low(layer_norm(resid, norm_gains[1], shifts[5]))
    hidden = linear(normed_two, up_w) + up_b
    hidden = low(
        0.5
        * hidden
        * (1.0 + jnp.tanh(0.7978845608 * (hidden + 0.044715 * hidden * hidden * hidden)))
    )
    return (resid + linear(hidden, down_w) + shifts[6]) * mask[..., None]


def block_params(pair, masks, params, index):
    mixer = spatial_mix if index == 0 else channel_mix
    return (block(pair[0], masks[0], params, mixer), block(pair[1], masks[1], params, mixer))


def crop_masks(extent, count):
    places = jnp.arange(WIN, dtype=jnp.int32)
    rows = places[None, :, None] < extent[:, 0][:, None, None]
    cols = places[None, None, :] < extent[:, 1][:, None, None]
    local_mask = jnp.logical_and(rows, cols).astype(jnp.float32)
    global_mask = jnp.ones((count, SIDE, SIDE), jnp.float32)
    return (global_mask, local_mask)


def body(
    global_tokens,
    local_tokens,
    crop_extent,
    conv_weight,
    vectors,
    gains,
    qkv_weight,
    proj_weight,
    fc1_weight,
    fc1_bias,
    fc2_weight,
    global_cotangent,
    local_cotangent,
):
    gathered = (
        lax.all_gather(conv_weight, "fsdp", axis=2, tiled=True),
        lax.all_gather(vectors, "fsdp", axis=2, tiled=True),
        lax.all_gather(gains, "fsdp", axis=2, tiled=True),
        lax.all_gather(qkv_weight, "fsdp", axis=1, tiled=True),
        lax.all_gather(proj_weight, "fsdp", axis=1, tiled=True),
        lax.all_gather(fc1_weight, "fsdp", axis=1, tiled=True),
        lax.all_gather(fc1_bias, "fsdp", axis=1, tiled=True),
        lax.all_gather(fc2_weight, "fsdp", axis=1, tiled=True),
    )
    weights = tuple((w.astype(jnp.float32) for w in gathered))
    masks = crop_masks(crop_extent, global_tokens.shape[0])
    glob = global_tokens.astype(jnp.float32)
    loc = local_tokens.astype(jnp.float32)
    cotangent = (global_cotangent.astype(jnp.float32), local_cotangent.astype(jnp.float32))
    start = (glob * masks[0][..., None], loc * masks[1][..., None])
    middle = block_params(start, masks, tuple((w[0] for w in weights)), 0)
    outputs = block_params(middle, masks, tuple((w[1] for w in weights)), 1)
    again = (
        lax.all_gather(conv_weight, "fsdp", axis=2, tiled=True),
        lax.all_gather(vectors, "fsdp", axis=2, tiled=True),
        lax.all_gather(gains, "fsdp", axis=2, tiled=True),
        lax.all_gather(qkv_weight, "fsdp", axis=1, tiled=True),
        lax.all_gather(proj_weight, "fsdp", axis=1, tiled=True),
        lax.all_gather(fc1_weight, "fsdp", axis=1, tiled=True),
        lax.all_gather(fc1_bias, "fsdp", axis=1, tiled=True),
        lax.all_gather(fc2_weight, "fsdp", axis=1, tiled=True),
    )
    weights_again = tuple((w.astype(jnp.float32) for w in again))

    def second_block(pair, params):
        return block_params(pair, masks, params, 1)

    def first_block(pair, params):
        return block_params(pair, masks, params, 0)

    unused, second_pull = jax.vjp(second_block, middle, tuple((w[1] for w in weights_again)))
    grad_middle, grad_second = second_pull(cotangent)
    unused_too, first_pull = jax.vjp(first_block, start, tuple((w[0] for w in weights_again)))
    grad_start, grad_first = first_pull(grad_middle)
    grad_g = grad_start[0] * masks[0][..., None]
    grad_l = grad_start[1] * masks[1][..., None]
    grad_w = tuple((jnp.stack([first, second]) for first, second in zip(grad_first, grad_second)))
    scattered = (
        lax.psum_scatter(
            grad_w[0].astype(jnp.bfloat16), "fsdp", scatter_dimension=2, tiled=True
        ).astype(jnp.float32),
        lax.psum_scatter(
            grad_w[1].astype(jnp.bfloat16), "fsdp", scatter_dimension=2, tiled=True
        ).astype(jnp.float32),
        lax.psum_scatter(
            grad_w[2].astype(jnp.bfloat16), "fsdp", scatter_dimension=2, tiled=True
        ).astype(jnp.float32),
        lax.psum_scatter(
            grad_w[3].astype(jnp.bfloat16), "fsdp", scatter_dimension=1, tiled=True
        ).astype(jnp.float32),
        lax.psum_scatter(
            grad_w[4].astype(jnp.bfloat16), "fsdp", scatter_dimension=1, tiled=True
        ).astype(jnp.float32),
        lax.psum_scatter(
            grad_w[5].astype(jnp.bfloat16), "fsdp", scatter_dimension=1, tiled=True
        ).astype(jnp.float32),
        lax.psum_scatter(
            grad_w[6].astype(jnp.bfloat16), "fsdp", scatter_dimension=1, tiled=True
        ).astype(jnp.float32),
        lax.psum_scatter(
            grad_w[7].astype(jnp.bfloat16), "fsdp", scatter_dimension=1, tiled=True
        ).astype(jnp.float32),
    )
    summed = (
        lax.psum(scattered[0].astype(jnp.bfloat16), "dp").astype(jnp.float32),
        lax.psum(scattered[1].astype(jnp.bfloat16), "dp").astype(jnp.float32),
        lax.psum(scattered[2].astype(jnp.bfloat16), "dp").astype(jnp.float32),
        lax.psum(scattered[3].astype(jnp.bfloat16), "dp").astype(jnp.float32),
        lax.psum(scattered[4].astype(jnp.bfloat16), "dp").astype(jnp.float32),
        lax.psum(scattered[5].astype(jnp.bfloat16), "dp").astype(jnp.float32),
        lax.psum(scattered[6].astype(jnp.bfloat16), "dp").astype(jnp.float32),
        lax.psum(scattered[7].astype(jnp.bfloat16), "dp").astype(jnp.float32),
    )
    return (
        outputs[0].astype(jnp.bfloat16),
        outputs[1].astype(jnp.bfloat16),
        grad_g,
        grad_l,
        summed[0],
        summed[1],
        summed[2],
        summed[3],
        summed[4],
        summed[5],
        summed[6],
        summed[7],
    )


def solution(mesh):
    return jax.shard_map(
        body,
        mesh=mesh,
        in_specs=(
            P(("dp", "fsdp"), None, None, None),
            P(("dp", "fsdp"), None, None, None),
            P(("dp", "fsdp"), None),
            P(None, None, "fsdp"),
            P(None, None, "fsdp"),
            P(None, None, "fsdp"),
            P(None, "fsdp", None),
            P(None, "fsdp", None),
            P(None, "fsdp", None),
            P(None, "fsdp"),
            P(None, "fsdp", None),
            P(("dp", "fsdp"), None, None, None),
            P(("dp", "fsdp"), None, None, None),
        ),
        out_specs=(
            P(("dp", "fsdp"), None, None, None),
            P(("dp", "fsdp"), None, None, None),
            P(("dp", "fsdp"), None, None, None),
            P(("dp", "fsdp"), None, None, None),
            P(None, None, "fsdp"),
            P(None, None, "fsdp"),
            P(None, None, "fsdp"),
            P(None, "fsdp", None),
            P(None, "fsdp", None),
            P(None, "fsdp", None),
            P(None, "fsdp"),
            P(None, "fsdp", None),
        ),
        check_vma=False,
    )
```

profile of v0, /device:TPU:0, one launch (start us, length us, event | category | flops | bytes accessed | tf_op | source)
XLA Modules:
  0.0 1068.1 jit_solution(3486684624478174462)
XLA Ops:
  10.8 10.5 all_gather.38
  24.5 9.5 all_gather.34
  34.0 8.6 all_gather.32
  42.6 9.6 all_gather.33
  52.4 35.7 %slice_reduce_fusion.16 = (f32[512]{0:T(512)}, f32[512]{0:T(512)}, f32[512]{0:T(512)}, f32[512]{0:T(512)}, f32[512]{0:T(512)}, /*index=5*/f32[512]{0:T(512)}, f3...) fusion(f32[2,9,512]{1,0,2:T(2,128)S(1)} %convert_element_type.310), kind=kLoop, calls=%fused_computation.426 | loop fusion | bytes 73728 | tf_op jit(solution)/shard_map/slice | solution.py:110
  88.3 27.6 %slice_reduce_fusion = (f32[512]{0:T(512)}, f32[512]{0:T(512)}, f32[512]{0:T(512)}, f32[512]{0:T(512)}, f32[512]{0:T(512)}, /*index=5*/f32[512]{0:T(512)}, f32[5...) fusion(f32[2,7,512]{1,0,2:T(2,128)S(1)} %convert_element_type.309), kind=kLoop, calls=%fused_computation.410 | loop fusion | bytes 57344 | tf_op jit(solution)/shard_map/slice | solution.py:174
  116.1 6.7 slice_reduce_fusion.2
  227.1 6.0 copy.247
  247.3 7.2 multiply_convert_fusion.5
  305.9 5.8 fusion.147
  395.4 7.0 fusion.145
  456.4 5.9 fusion.146
  535.0 7.1 fusion.144
  621.5 5.4 reshape.954
  684.8 5.8 fusion.165
  718.0 7.6 fusion.129
  754.0 24.4 %reduce-scatter.21.cloned.1.call-done = bf16[2,64,2048]{2,1,0:T(8,128)(2,1)} async-done(((bf16[2,512,2048]{2,1,0:T(8,128)(2,1)}), bf16[2,64,2048]{2,1,0:T(8,128)(2,1)}) %reduce-scatter.21.cloned.1.call-update) | async-done | bytes 524304 | tf_op jit(solution)/shard_map/reduce_scatter | solution.py:265
  778.4 54.7 %reduce-scatter.23.cloned.1.call-done = bf16[2,256,512]{2,1,0:T(8,128)(2,1)} async-done(((bf16[2,2048,512]{2,1,0:T(8,128)(2,1)}), bf16[2,256,512]{2,1,0:T(8,128)(2,1)}) %reduce-scatter.23.cloned.1.call-update) | async-done | bytes 524304 | tf_op jit(solution)/shard_map/reduce_scatter | solution.py:271
  848.6 21.2 %reduce-scatter.29.cloned.1.call-done = bf16[64,4]{1,0:T(8,128)(2,1)} async-done(((bf16[512,4]{1,0:T(8,128)(2,1)}), bf16[64,4]{1,0:T(8,128)(2,1)}) %reduce-scatter.29.cloned.1.call-update) | async-done | bytes 528
  870.7 36.8 %reduce-scatter.31.cloned.1.call-done = bf16[256,2]{1,0:T(8,128)(2,1)} async-done(((bf16[2048,2]{1,0:T(8,128)(2,1)}), bf16[256,2]{1,0:T(8,128)(2,1)}) %reduce-scatter.31.cloned.1.call-update) | async-done | bytes 1040
  908.4 35.8 %reduce-scatter.27.cloned.1.call-done = bf16[64,14]{1,0:T(8,128)(2,1)} async-done(((bf16[512,14]{1,0:T(8,128)(2,1)}), bf16[64,14]{1,0:T(8,128)(2,1)}) %reduce-scatter.27.cloned.1.call-update) | async-done | bytes 1808
  945.1 36.0 %reduce-scatter.25.cloned.1.call-done = bf16[64,18]{1,0:T(8,128)(2,1)} async-done(((bf16[512,18]{1,0:T(8,128)(2,1)}), bf16[64,18]{1,0:T(8,128)(2,1)}) %reduce-scatter.25.cloned.1.call-update) | async-done | bytes 2320
  981.9 19.2 %all-reduce.124 = (bf16[2,9,64]{2,1,0:T(8,128)(2,1)S(1)}, bf16[2,7,64]{2,1,0:T(8,128)(2,1)S(1)}, bf16[2,2,64]{2,1,0:T(2,128)(2,1)S(1)}, bf16[2,256]{1,0:T(2,128)(2,1)S(1)}) all-reduce(bf16[2,9,64]{2,1,0:T(8,128)(2,1)S(1)} %copy.345, bf16[2,7,64]{2,1,0:T(8,128)(2,1)S(1)} %copy.347, ...), channel_id=1, replica_groups=mesh['dp'=4,'fsdp'=8] {'dp'}, use_global_device_ids=true, to_apply=%region_89.90 | all-reduce | flops 2816 | bytes 11264 | tf_op jit(solution)/shard_map/psum | solution.py:276
  1003.5 50.8 %all-reduce.128.cloned.1.call-done = (bf16[2,64,1536]{2,1,0:T(8,128)(2,1)}, bf16[2,64,512]{2,1,0:T(8,128)(2,1)}, bf16[2,64,2048]{2,1,0:T(8,128)(2,1)}, bf16[2,256,512]{2,1,0:T(8,128)(2,1)}) async-done(((bf16[2,64,1536]{2,1,0:T(8,128)(2,1)}, bf16[2,64,512]{2,1,0:T(8,128)(2,1)}, bf16[2,64,2048]{2,1,0:T(8,128)(2,1)}, bf16[2,256,512]{2,1,0:T(8,128)(2,1)}), (bf16[2,64,1536]{2,1,0:T(8,128)(2,1)}, ...) | async-done | bytes 1572880 | tf_op jit(solution)/shard_map/psum | solution.py:279
  (1106 shorter events, 604.7 us)
Async XLA Ops:
  7.2 121.2 %all-gather.7.cloned.1.call-start = ((), (), s32[]{:S(2)}) async-start(), calls=%async_computation.9 | async-start | bytes 1179648 | tf_op jit(solution)/shard_map/all_gather | solution.py:211
  7.9 123.0 %all-gather.5.cloned.1.call-start = ((), (), s32[]{:S(2)}) async-start(), calls=%async_computation.8 | async-start | bytes 3538944 | tf_op jit(solution)/shard_map/all_gather | solution.py:210
  8.7 238.7 %all-gather.9.cloned.1.call-start = ((), (), s32[]{:S(2)}) async-start(), calls=%async_computation.10 | async-start | bytes 4718592 | tf_op jit(solution)/shard_map/all_gather | solution.py:212
  9.4 245.2 %all-gather.11.cloned.1.call-start = ((), (), s32[]{:S(2)}) async-start(), calls=%async_computation.11 | async-start | bytes 4718592 | tf_op jit(solution)/shard_map/all_gather | solution.py:214
  10.0 744.1 %reduce-scatter.19.cloned.1.call-start = ((), (), s32[]{:S(2)}) async-start(), calls=%async_computation.13 | async-start | bytes 1179648 | tf_op jit(solution)/shard_map/reduce_scatter | solution.py:262
  22.0 430.7 %copy-start.88 = (f32[9,7,7]{2,1,0:T(8,128)}, f32[9,7,7]{2,1,0:T(8,128)S(1)}, u32[]{:S(2)}) copy-start(f32[9,7,7]{2,1,0:T(8,128)S(1)} %and_convert_fusion) | copy-start | bytes 5296
  22.1 65.9 %copy-start.199 = (f32[9,49]{1,0:T(8,128)}, f32[9,49]{1,0:T(8,128)S(1)}, u32[]{:S(2)}) copy-start(f32[9,49]{1,0:T(8,128)S(1)} %reshape.964) | copy-start | bytes 5296
  22.1 176.0 %copy-start.204 = (pred[9,49]{1,0:T(8,128)(4,1)}, pred[9,49]{1,0:T(8,128)(4,1)S(1)}, u32[]{:S(2)}) copy-start(pred[9,49]{1,0:T(8,128)(4,1)S(1)} %broadcast_compare_fusion.1) | copy-start | bytes 1327
  122.8 121.4 %copy-start.201 = (f32[512]{0:T(512)}, f32[512]{0:T(512)S(1)}, u32[]{:S(2)}) copy-start(f32[512]{0:T(512)S(1)} %get-tuple-element.148) | copy-start | bytes 6148
  124.2 89.1 %copy-start.9 = (f32[9,7,7,512]{3,2,1,0:T(8,128)}, f32[9,7,7,512]{3,2,1,0:T(8,128)S(1)}, u32[]{:S(2)}) copy-start(f32[9,7,7,512]{3,2,1,0:T(8,128)S(1)} %get-tuple-element.207) | copy-start | bytes 2709508
  127.6 114.4 %copy-start.5 = (f32[3,14,14,512]{3,2,1,0:T(8,128)}, f32[3,14,14,512]{3,2,1,0:T(8,128)S(1)}, u32[]{:S(2)}) copy-start(f32[3,14,14,512]{3,2,1,0:T(8,128)S(1)} %get-tuple-element.211) | copy-start | bytes 3612676
  198.6 47.4 %copy-start.132 = (f32[9,16,49]{2,1,0:T(8,128)}, f32[9,16,49]{2,1,0:T(8,128)S(1)}, u32[]{:S(2)}) copy-start(f32[9,16,49]{2,1,0:T(8,128)S(1)} %fusion.64) | copy-start | bytes 84676
  215.4 39.2 %copy-start.14 = (f32[9,7,7,512]{3,2,1,0:T(8,128)}, f32[9,7,7,512]{3,2,1,0:T(8,128)S(1)}, u32[]{:S(2)}) copy-start(f32[9,7,7,512]{3,2,1,0:T(8,128)S(1)} %get-tuple-element.295) | copy-start | bytes 2709508
  315.2 132.4 %copy-start.24 = (f32[9,7,7,512]{3,2,1,0:T(8,128)}, f32[9,7,7,512]{3,2,1,0:T(8,128)S(1)}, u32[]{:S(2)}) copy-start(f32[9,7,7,512]{3,2,1,0:T(8,128)S(1)} %get-tuple-element.197) | copy-start | bytes 2709508
  344.5 43.9 %copy-start.3 = (f32[3,14,14,512]{3,2,1,0:T(8,128)}, f32[3,14,14,512]{3,2,1,0:T(8,128)S(1)}, u32[]{:S(2)}) copy-start(f32[3,14,14,512]{3,2,1,0:T(8,128)S(1)} %get-tuple-element.209) | copy-start | bytes 3612676
  616.4 137.6 %reduce-scatter.17.cloned.1.call-start = ((), (), s32[]{:S(2)}) async-start(), calls=%async_computation.12 | async-start | bytes 3538944 | tf_op jit(solution)/shard_map/reduce_scatter | solution.py:259
  676.4 102.0 %reduce-scatter.21.cloned.1.call-start = ((), (), s32[]{:S(2)}) async-start(), calls=%async_computation.14 | async-start | bytes 4718592 | tf_op jit(solution)/shard_map/reduce_scatter | solution.py:265
  690.6 142.6 %reduce-scatter.23.cloned.1.call-start = ((), (), s32[]{:S(2)}) async-start(), calls=%async_computation.15 | async-start | bytes 4718592 | tf_op jit(solution)/shard_map/reduce_scatter | solution.py:271
  703.1 166.7 %reduce-scatter.29.cloned.1.call-start = ((), (), s32[]{:S(2)}) async-start(), calls=%async_computation.18 | async-start | bytes 147456
  740.6 166.9 %reduce-scatter.31.cloned.1.call-start = ((), (), s32[]{:S(2)}) async-start(), calls=%async_computation.19 | async-start | bytes 589824
  742.5 201.7 %reduce-scatter.27.cloned.1.call-start = ((), (), s32[]{:S(2)}) async-start(), calls=%async_computation.17 | async-start | bytes 147456
  745.2 235.9 %reduce-scatter.25.cloned.1.call-start = ((), (), s32[]{:S(2)}) async-start(), calls=%async_computation.16 | async-start | bytes 147456
  747.4 306.9 %all-reduce.128.cloned.1.call-start = ((), (), s32[]{:S(2)}) async-start(), calls=%async_computation.20 | async-start | bytes 3145728 | tf_op jit(solution)/shard_map/psum | solution.py:279
  754.0 79.2 %copy-start.55 = (f32[9,7,7,512]{3,2,1,0:T(8,128)S(1)}, f32[9,7,7,512]{3,2,1,0:T(8,128)}, u32[]{:S(2)}) copy-start(f32[9,7,7,512]{3,2,1,0:T(8,128)} %copy-done.54) | copy-start | bytes 2709508
  (361 other events, 1752.1 us)
Sparse Core Ops, SparseCore 0:
  9.9 26.5 all-gather.6
  38.4 32.9 all-gather.4
  73.3 36.7 all-gather.8
  111.9 36.7 all-gather.10
  616.6 36.5 reduce-scatter.18
  676.6 46.7 reduce-scatter.16
  727.1 51.2 reduce-scatter.20
  781.8 51.3 reduce-scatter.22
  836.5 33.3 reduce-scatter.28
  873.3 34.1 reduce-scatter.30
  910.8 33.3 reduce-scatter.26
  947.6 33.3 reduce-scatter.24
  983.8 70.4 all-reduce.127
where the time goes:
time: 1080 us; the launch traced here: 1070 us
  local copies, waits for them, and re-layouts  381 us (35%)
  waiting for transfers between devices  262 us (24%)
  matrix products  202 us (19%)
  other arithmetic  145 us (13%)
  blocking collectives  57.3 us (5%)
  between operations  18.9 us (2%)
    dot_general x48, matrix products, contract(): return product(first_operand, second_operand)  138 us
    unnamed x17, waiting for transfers between devices  132 us
    dot_general x24, matrix products, product_value(): jnp.einsum(forms[0], first.astype(jnp.bfloat16), second.astype(jnp.bfloat...  64.6 us
    convert_element_type x20, local copies, waits for them, and re-layouts, product_value(): second.astype(jnp.bfloat16)  60 us
    reduce_scatter x1, waiting for transfers between devices, body(): lax.psum_scatter(grad_w[7].astype(jnp.bfloat16), 'fsdp', scatter_dimensio...  54.7 us
    psum x1, waiting for transfers between devices, body(): lax.psum(scattered[3].astype(jnp.bfloat16), 'dp').astype(jnp.float32)  50.8 us
    transpose x11, local copies, waits for them, and re-layouts, contract(): return product(first_operand, second_operand)  45.6 us
    unnamed x763, local copies, waits for them, and re-layouts  39.5 us
  transfers between devices with their start and end apart: 13, of which 7 were waited for; matrix products, arithmetic and copies ran while one was open for 33% of the time, Pallas kernels for 0%

commit v1 on v0

v1 whole, which is shorter than its diff:
```python
import functools

import jax
import jax.numpy as jnp
from jax import lax
from jax.experimental import pallas as pl
from jax.experimental.pallas import tpu as pltpu
from jax.sharding import PartitionSpec as P

BF = jnp.bfloat16
F32 = jnp.float32
C = 512
FF = 2048
HEAD = 32
WIN = 7
SIDE = 14
CELL = 64
LANES = 128
GROUPS = C // LANES
PER = LANES // HEAD
EPS = 1e-5
SCALE = HEAD ** -0.5
VMEM = pl.BlockSpec(memory_space=pltpu.VMEM)
NT = (((1,), (1,)), ((), ()))
TN = (((0,), (0,)), ((), ()))
K_ROW, V_ROW, G_ROW, B_ROW, SMALL = 0, 9, 16, 18, 22


def mm(a, b):
    return jnp.dot(a, b, preferred_element_type=F32)


def mm_nt(a, b):
    return lax.dot_general(a, b, NT, preferred_element_type=F32)


def mm_tn(a, b):
    return lax.dot_general(a, b, TN, preferred_element_type=F32)


def call(kernel, outs, ins, scratch=(), limit=60):
    return pl.pallas_call(
        kernel,
        out_shape=outs,
        in_specs=[VMEM] * len(ins),
        out_specs=[VMEM] * len(outs),
        scratch_shapes=list(scratch),
        compiler_params=pltpu.CompilerParams(vmem_limit_bytes=limit * 2**20),
    )(*ins)


def shape(dims, kind):
    return jax.ShapeDtypeStruct(dims, kind)


def wide(m):
    return jnp.concatenate([m] * GROUPS, axis=1)


def fold8(v):
    return jnp.sum(v.reshape(v.shape[0] // 8, 8, v.shape[1]), axis=0)


def norm_parts(x):
    center = jnp.sum(x, axis=-1, keepdims=True) * (1.0 / C)
    xc = x - center
    var = jnp.sum(xc * xc, axis=-1, keepdims=True) * (1.0 / C)
    rstd = lax.rsqrt(var + EPS)
    return xc * rstd, rstd


def norm_back(dn, xhat, rstd, gain):
    gp = dn * gain
    m1 = jnp.sum(gp, axis=-1, keepdims=True) * (1.0 / C)
    m2 = jnp.sum(gp * xhat, axis=-1, keepdims=True) * (1.0 / C)
    return rstd * (gp - m1 - xhat * m2)


def head_masks(rows):
    lane = lax.broadcasted_iota(jnp.int32, (rows, LANES), 1) // HEAD
    return [lane == h for h in range(PER)]


def spread(v, masks):
    zero = jnp.zeros_like(v)
    return jnp.concatenate([jnp.where(m, v, zero) for m in masks], axis=0)


def gather_heads(full, masks):
    n = full.shape[0] // PER
    out = full[3 * n :]
    for h in (2, 1, 0):
        out = jnp.where(masks[h], full[h * n : (h + 1) * n], out)
    return out


def shifted_cols(left, right, j, step):
    if step == 0:
        return left, right
    if step == 1:
        return (
            jnp.where(j == 6, pltpu.roll(right, 6, 1), pltpu.roll(left, 7, 1)),
            pltpu.roll(right, 7, 1),
        )
    return (
        pltpu.roll(left, 1, 1),
        jnp.where(j == 0, pltpu.roll(left, 2, 1), pltpu.roll(right, 1, 1)),
    )


def canvas(ref, crop, lanes):
    base = crop * 32
    parts = [ref[pl.ds(base + 8 * w, 7), :, lanes] for w in range(4)]
    left = jnp.concatenate([parts[0], parts[2]], axis=0)
    right = jnp.concatenate([parts[1], parts[3]], axis=0)
    return left, right


def put_canvas(ref, crop, lanes, left, right, mask_ref):
    base = crop * 32
    zero = jnp.zeros((1, 8, LANES), F32)
    for w in range(4):
        side = right if w % 2 else left
        half = side[(w // 2) * 7 : (w // 2) * 7 + 7]
        rows = pl.ds(base + 8 * w, 8)
        ref[rows, :, lanes] = jnp.concatenate([half, zero], axis=0) * mask_ref[rows]


def conv_forward(u_ref, c_ref, small_ref, mask_ref, globals_, locals_):
    j14 = lax.broadcasted_iota(jnp.int32, (14, 8, LANES), 1)
    for g in range(GROUPS):
        lanes = pl.ds(g * LANES, LANES)
        taps = [small_ref[K_ROW + t : K_ROW + t + 1, lanes][None] for t in range(9)]
        shift = small_ref[V_ROW : V_ROW + 1, lanes][None]

        @pl.loop(0, globals_)
        def _(crop):
            left, right = canvas(u_ref, crop, lanes)
            zero = jnp.zeros((1, 8, LANES), F32)
            acc = [left + shift, right + shift]
            for e in (-1, 0, 1):
                for s, side in enumerate(shifted_cols(left, right, j14, e)):
                    tall = jnp.concatenate([zero, side, zero], axis=0)
                    for a in (-1, 0, 1):
                        acc[s] = acc[s] + taps[3 * (a + 1) + e + 1] * tall[1 + a : 15 + a]
            put_canvas(c_ref, crop, lanes, acc[0], acc[1], mask_ref)

        @pl.loop(0, locals_)
        def _(n):
            rows = pl.ds(globals_ * 32 + n * 8, 8)
            u = u_ref[rows, :, lanes]
            acc = u + shift
            for e in (-1, 0, 1):
                side = u if e == 0 else pltpu.roll(u, 7 if e == 1 else 1, 1)
                for a in (-1, 0, 1):
                    moved = side if a == 0 else jnp.roll(side, -a, axis=0)
                    acc = acc + taps[3 * (a + 1) + e + 1] * moved
            c_ref[rows, :, lanes] = acc * mask_ref[rows]


def conv_backward(d_ref, u_ref, du_ref, small_ref, acc_ref, globals_, locals_):
    j14 = lax.broadcasted_iota(jnp.int32, (14, 8, LANES), 1)
    for g in range(GROUPS):
        lanes = pl.ds(g * LANES, LANES)
        taps = [small_ref[K_ROW + t : K_ROW + t + 1, lanes][None] for t in range(9)]
        nothing = tuple(jnp.zeros((8, LANES), F32) for _ in range(10))

        def one_crop(crop, sums):
            sums = list(sums)
            left, right = canvas(d_ref, crop, lanes)
            own = canvas(u_ref, crop, lanes)
            zero = jnp.zeros((1, 8, LANES), F32)
            acc = [left, right]
            sums[9] = sums[9] + jnp.sum(left + right, axis=0)
            for e in (-1, 0, 1):
                for s, side in enumerate(shifted_cols(left, right, j14, -e)):
                    tall = jnp.concatenate([zero, side, zero], axis=0)
                    for a in (-1, 0, 1):
                        t = 3 * (a + 1) + e + 1
                        moved = tall[1 - a : 15 - a]
                        acc[s] = acc[s] + taps[t] * moved
                        sums[t] = sums[t] + jnp.sum(own[s] * moved, axis=0)
            base = crop * 32
            for w in range(4):
                side = acc[w % 2]
                half = side[(w // 2) * 7 : (w // 2) * 7 + 7]
                du_ref[pl.ds(base + 8 * w, 8), :, lanes] = jnp.concatenate([half, zero], axis=0)
            return tuple(sums)

        def one_local(n, sums):
            sums = list(sums)
            rows = pl.ds(globals_ * 32 + n * 8, 8)
            d = d_ref[rows, :, lanes]
            own = u_ref[rows, :, lanes]
            acc = d
            sums[9] = sums[9] + jnp.sum(d, axis=0)
            for e in (-1, 0, 1):
                side = d if e == 0 else pltpu.roll(d, 7 if e == -1 else 1, 1)
                for a in (-1, 0, 1):
                    t = 3 * (a + 1) + e + 1
                    moved = side if a == 0 else jnp.roll(side, a, axis=0)
                    acc = acc + taps[t] * moved
                    sums[t] = sums[t] + jnp.sum(own * moved, axis=0)
            du_ref[rows, :, lanes] = acc
            return tuple(sums)

        sums = lax.fori_loop(0, globals_, one_crop, nothing)
        sums = lax.fori_loop(0, locals_, one_local, sums)
        for t in range(10):
            acc_ref[t, :, lanes] = sums[t]


def spatial_forward(q_ref, k_ref, v_ref, mask_ref, o_ref, p_ref, windows):
    masks = head_masks(CELL)

    @pl.loop(0, windows)
    def _(w):
        rows = pl.ds(w * CELL, CELL)
        m = mask_ref[rows, :]
        valid = jnp.concatenate([m, m], axis=1) > 0.5
        for g in range(GROUPS):
            lanes = pl.ds(g * LANES, LANES)
            s = mm_nt(k_ref[rows, lanes], spread(q_ref[rows, lanes], masks))
            s = jnp.where(valid, s * SCALE, -1e9)
            e = jnp.exp(s - jnp.max(s, axis=0, keepdims=True))
            p = (e / jnp.sum(e, axis=0, keepdims=True)).astype(BF)
            p_ref[w, g] = p
            o_ref[rows, lanes] = gather_heads(mm_tn(p, v_ref[rows, lanes]), masks).astype(BF)


def spatial_backward(q_ref, k_ref, v_ref, p_ref, do_ref, dq_ref, dk_ref, dv_ref, acc_ref, windows):
    masks = head_masks(CELL)

    @pl.loop(0, windows)
    def _(w):
        rows = pl.ds(w * CELL, CELL)
        for g in range(GROUPS):
            lanes = pl.ds(g * LANES, LANES)
            p = p_ref[w, g]
            dos = spread(do_ref[rows, lanes], masks)
            dp = mm_nt(v_ref[rows, lanes], dos)
            pf = p.astype(F32)
            total = jnp.sum(pf * dp, axis=0, keepdims=True)
            ds = (pf * (dp - total) * SCALE).astype(BF)
            dv = mm(p, dos)
            dk = mm(ds, spread(q_ref[rows, lanes], masks))
            dq = gather_heads(mm_tn(ds, k_ref[rows, lanes]), masks)
            acc_ref[0, :, lanes] += fold8(dq)
            acc_ref[1, :, lanes] += fold8(dv)
            dq_ref[rows, lanes] = dq.astype(BF)
            dk_ref[rows, lanes] = dk.astype(BF)
            dv_ref[rows, lanes] = dv.astype(BF)


def same_head():
    a = lax.broadcasted_iota(jnp.int32, (LANES, LANES), 0) // HEAD
    b = lax.broadcasted_iota(jnp.int32, (LANES, LANES), 1) // HEAD
    return a == b


def over_crops(globals_, locals_, step):
    @pl.loop(0, globals_)
    def _(n):
        step(n, n * 4 * CELL, 4 * CELL)

    @pl.loop(0, locals_)
    def _(n):
        step(globals_ + n, globals_ * 4 * CELL + n * CELL, CELL)


def channel_forward(q_ref, k_ref, v_ref, mask_ref, o_ref, p_ref, globals_, locals_):
    same = same_head()

    def step(n, start, count):
        rows = pl.ds(start, count)
        m = mask_ref[rows, :].astype(BF)
        for g in range(GROUPS):
            lanes = pl.ds(g * LANES, LANES)
            s = mm_tn(v_ref[rows, lanes], k_ref[rows, lanes] * m)
            s = jnp.where(same, s * SCALE, -jnp.inf)
            e = jnp.exp(s - jnp.max(s, axis=0, keepdims=True))
            p = (e / jnp.sum(e, axis=0, keepdims=True)).astype(BF)
            p_ref[n, g] = p
            o_ref[rows, lanes] = mm(q_ref[rows, lanes], p).astype(BF)

    over_crops(globals_, locals_, step)


def channel_backward(
    q_ref, k_ref, v_ref, mask_ref, p_ref, do_ref, dq_ref, dk_ref, dv_ref, acc_ref, globals_, locals_
):
    def step(n, start, count):
        rows = pl.ds(start, count)
        mf = mask_ref[rows, :]
        m = mf.astype(BF)
        for g in range(GROUPS):
            lanes = pl.ds(g * LANES, LANES)
            p = p_ref[n, g]
            do = do_ref[rows, lanes]
            dq = mm_nt(do, p)
            dp = mm_tn(q_ref[rows, lanes], do)
            pf = p.astype(F32)
            total = jnp.sum(pf * dp, axis=0, keepdims=True)
            ds = (pf * (dp - total) * SCALE).astype(BF)
            dk = mm(v_ref[rows, lanes], ds) * mf
            dv = mm_nt(k_ref[rows, lanes] * m, ds)
            acc_ref[0, :, lanes] += fold8(dq)
            acc_ref[1, :, lanes] += fold8(dv)
            dq_ref[rows, lanes] = dq.astype(BF)
            dk_ref[rows, lanes] = dk.astype(BF)
            dv_ref[rows, lanes] = dv.astype(BF)

    over_crops(globals_, locals_, step)


def attention_forward(sizes, kind, u, mask, small, weights):
    globals_, locals_, shards = sizes
    windows = 4 * globals_ + locals_
    rows = windows * CELL
    chunk = rows // 3
    part = C // shards

    def kernel(u_ref, mask_ref, small_ref, w_ref, r_ref, c_ref, n_ref, q_ref, k_ref, v_ref, o_ref, p_ref):
        conv_forward(u_ref, c_ref, small_ref, mask_ref.reshape(windows * 8, 8, LANES), globals_, locals_)
        gain = small_ref[G_ROW : G_ROW + 1]
        shift = small_ref[V_ROW + 1 : V_ROW + 2]

        @pl.loop(0, windows)
        def _(w):
            x = c_ref[pl.ds(w * 8, 8)].reshape(CELL, C)
            xhat, _ = norm_parts(x)
            n_ref[pl.ds(w * CELL, CELL), :] = (xhat * gain + shift).astype(BF)

        def weight(i):
            return w_ref[:, i * part : (i + 1) * part, :].reshape(C, C)

        @pl.loop(0, 3)
        def _(i):
            here = pl.ds(i * chunk, chunk)
            n1 = n_ref[here, :]
            q_ref[here, :] = (mm(n1, weight(0)) + small_ref[V_ROW + 2 : V_ROW + 3]).astype(BF)
            k_ref[here, :] = mm(n1, weight(1)).astype(BF)
            v_ref[here, :] = (mm(n1, weight(2)) + small_ref[V_ROW + 3 : V_ROW + 4]).astype(BF)

        if kind == 0:
            spatial_forward(q_ref, k_ref, v_ref, mask_ref, o_ref, p_ref, windows)
        else:
            channel_forward(q_ref, k_ref, v_ref, mask_ref, o_ref, p_ref, globals_, locals_)

        @pl.loop(0, 3)
        def _(i):
            here = pl.ds(i * chunk, chunk)
            c = c_ref[pl.ds(i * (chunk // 8), chunk // 8)].reshape(chunk, C)
            r_ref[here, :] = c + mm(o_ref[here, :], weight(3)) + small_ref[V_ROW + 4 : V_ROW + 5]

    low = shape((rows, C), BF)
    probs = (windows, GROUPS, CELL, PER * CELL) if kind == 0 else (globals_ + locals_, GROUPS, LANES, LANES)
    outs = [shape((rows, C), F32), shape((windows * 8, 8, C), F32), low, low, low, low, low, shape(probs, BF)]
    return call(kernel, outs, (u, mask, small, weights))


def ffn_forward(sizes, r, mask, small, weights):
    globals_, locals_, shards = sizes
    windows = 4 * globals_ + locals_
    rows = windows * CELL
    chunk = rows // 3
    part = C // shards
    deep = FF // shards

    def kernel(r_ref, mask_ref, small_ref, w_ref, x_ref, n_ref, g_ref, s_ref):
        gain = small_ref[G_ROW + 1 : G_ROW + 2]
        shift = small_ref[V_ROW + 5 : V_ROW + 6]

        @pl.loop(0, windows)
        def _(w):
            here = pl.ds(w * CELL, CELL)
            xhat, _ = norm_parts(r_ref[here, :])
            n_ref[here, :] = (xhat * gain + shift).astype(BF)

        @pl.loop(0, 3)
        def _(i):
            here = pl.ds(i * chunk, chunk)
            n2 = n_ref[here, :]
            for t in range(FF // C):
                w = w_ref[:, t * part : (t + 1) * part, :].reshape(C, C)
                h = mm(n2, w) + small_ref[B_ROW + t : B_ROW + t + 1]
                h2 = h * h
                a = 0.5 + 0.5 * jnp.tanh(h * (0.7978845608 + (0.7978845608 * 0.044715) * h2))
                g = h * a
                slope = a + (2.0 * g) * (1.0 - a) * (0.7978845608 + (3 * 0.7978845608 * 0.044715) * h2)
                g_ref[here, t * C : (t + 1) * C] = g.astype(BF)
                s_ref[here, t * C : (t + 1) * C] = slope.astype(BF)
            w = w_ref[:, 4 * part :, :].reshape(FF, C)
            y = r_ref[here, :] + mm(g_ref[here, :], w) + small_ref[V_ROW + 6 : V_ROW + 7]
            x_ref[here, :] = y * wide(mask_ref[here, :])

    high = shape((rows, FF), BF)
    outs = [shape((rows, C), F32), shape((rows, C), BF), high, high]
    return call(kernel, outs, (r, mask, small, weights))


def ffn_backward(sizes, dy, r, n2, g, slope, mask, small, weights):
    globals_, locals_, shards = sizes
    windows = 4 * globals_ + locals_
    rows = windows * CELL
    chunk = rows // 3
    part = C // shards
    deep = FF // shards

    def kernel(dy_ref, r_ref, n_ref, g_ref, s_ref, mask_ref, small_ref, w_ref, dr_ref, dw_ref, ds_ref, dyl, dh, acc, acc1):
        acc[...] = jnp.zeros_like(acc)
        acc1[...] = jnp.zeros_like(acc1)

        @pl.loop(0, windows)
        def _(w):
            here = pl.ds(w * CELL, CELL)
            d = dy_ref[here, :] * wide(mask_ref[here, :])
            dyl[here, :] = d.astype(BF)
            acc[2] += fold8(d)

        @pl.loop(0, 3)
        def _(i):
            here = pl.ds(i * chunk, chunk)
            for t in range(FF // C):
                cols = slice(t * C, (t + 1) * C)
                w2 = w_ref[t * C // deep : (t + 1) * C // deep, 4 * part :, :].reshape(C, C)
                d = mm_nt(dyl[here, :], w2) * s_ref[here, cols].astype(F32)
                acc1[:, cols] += fold8(d)
                dh[here, cols] = d.astype(BF)
            dn = None
            for t in range(FF // C):
                w1 = w_ref[:, t * part : (t + 1) * part, :].reshape(C, C)
                one = mm_nt(dh[here, t * C : (t + 1) * C], w1)
                dn = one if dn is None else dn + one
            dr_ref[here, :] = dn

        gain = small_ref[G_ROW + 1 : G_ROW + 2]

        @pl.loop(0, windows)
        def _(w):
            here = pl.ds(w * CELL, CELL)
            dn = dr_ref[here, :]
            xhat, rstd = norm_parts(r_ref[here, :])
            acc[0] += fold8(dn * xhat)
            acc[1] += fold8(dn)
            dr_ref[here, :] = norm_back(dn, xhat, rstd, gain) + dy_ref[here, :] * wide(mask_ref[here, :])

        for t in range(FF // C):
            cols = slice(t * C, (t + 1) * C)
            dw_ref[:, t * part : (t + 1) * part, :] = (
                mm_tn(n_ref[...], dh[:, cols]).astype(BF).reshape(shards, part, C)
            )
            dw_ref[t * C // deep : (t + 1) * C // deep, 4 * part :, :] = (
                mm_tn(g_ref[:, cols], dyl[...]).astype(BF).reshape(C // deep, deep, C)
            )
        for i in range(3):
            ds_ref[i : i + 1, :] = jnp.sum(acc[i], axis=0, keepdims=True)
        for t in range(FF // C):
            ds_ref[3 + t : 4 + t, :] = jnp.sum(acc1[:, t * C : (t + 1) * C], axis=0, keepdims=True)
        ds_ref[7:8, :] = jnp.zeros((1, C), F32)

    outs = [shape((rows, C), F32), shape((shards, 4 * part + deep, C), BF), shape((8, C), F32)]
    scratch = [
        pltpu.VMEM((rows, C), BF),
        pltpu.VMEM((rows, FF), BF),
        pltpu.VMEM((3, 8, C), F32),
        pltpu.VMEM((8, FF), F32),
    ]
    return call(kernel, outs, (dy, r, n2, g, slope, mask, small, weights), scratch)


def attention_backward(sizes, kind, dr, u, c, n1, q, k, v, o, p, mask, small, weights):
    globals_, locals_, shards = sizes
    windows = 4 * globals_ + locals_
    rows = windows * CELL
    chunk = rows // 3
    part = C // shards

    def kernel(
        dr_ref, u_ref, c_ref, n_ref, q_ref, k_ref, v_ref, o_ref, p_ref, mask_ref, small_ref, w_ref,
        du_ref, dw_ref, ds_ref, drl, do, dq, dk, dv, dn, acc, acck,
    ):
        acc[...] = jnp.zeros_like(acc)

        def weight(i):
            return w_ref[:, i * part : (i + 1) * part, :].reshape(C, C)

        @pl.loop(0, windows)
        def _(w):
            here = pl.ds(w * CELL, CELL)
            d = dr_ref[here, :]
            drl[here, :] = d.astype(BF)
            acc[4] += fold8(d)

        @pl.loop(0, 3)
        def _(i):
            here = pl.ds(i * chunk, chunk)
            do[here, :] = mm_nt(drl[here, :], weight(3)).astype(BF)

        if kind == 0:
            spatial_backward(q_ref, k_ref, v_ref, p_ref, do, dq, dk, dv, acc, windows)
        else:
            channel_backward(
                q_ref, k_ref, v_ref, mask_ref, p_ref, do, dq, dk, dv, acc, globals_, locals_
            )

        @pl.loop(0, 3)
        def _(i):
            here = pl.ds(i * chunk, chunk)
            total = mm_nt(dq[here, :], weight(0)) + mm_nt(dk[here, :], weight(1)) + mm_nt(dv[here, :], weight(2))
            dn[pl.ds(i * (chunk // 8), chunk // 8)] = total.reshape(chunk // 8, 8, C)

        gain = small_ref[G_ROW : G_ROW + 1]

        @pl.loop(0, windows)
        def _(w):
            here = pl.ds(w * CELL, CELL)
            tiles = pl.ds(w * 8, 8)
            d = dn[tiles].reshape(CELL, C)
            xhat, rstd = norm_parts(c_ref[tiles].reshape(CELL, C))
            acc[2] += fold8(d * xhat)
            acc[3] += fold8(d)
            dc = norm_back(d, xhat, rstd, gain) + dr_ref[here, :]
            dn[tiles] = (dc * wide(mask_ref[here, :])).reshape(8, 8, C)

        conv_backward(dn, u_ref, du_ref, small_ref, acck, globals_, locals_)

        for i, (left, right) in enumerate(((n_ref, dq), (n_ref, dk), (n_ref, dv), (o_ref, drl))):
            dw_ref[:, i * part : (i + 1) * part, :] = (
                mm_tn(left[...], right[...]).astype(BF).reshape(shards, part, C)
            )
        for t in range(10):
            ds_ref[t : t + 1, :] = jnp.sum(acck[t], axis=0, keepdims=True)
        for t in range(5):
            ds_ref[10 + t : 11 + t, :] = jnp.sum(acc[t], axis=0, keepdims=True)
        ds_ref[15:16, :] = jnp.zeros((1, C), F32)

    outs = [shape((windows * 8, 8, C), F32), shape((shards, 4 * part, C), BF), shape((16, C), F32)]
    low = pltpu.VMEM((rows, C), BF)
    scratch = [
        low, low, low, low, low,
        pltpu.VMEM((windows * 8, 8, C), F32),
        pltpu.VMEM((5, 8, C), F32),
        pltpu.VMEM((10, 8, C), F32),
    ]
    return call(kernel, outs, (dr, u, c, n1, q, k, v, o, p, mask, small, weights), scratch)


def to_cells(glob, loc):
    count = glob.shape[0]
    wins = glob.reshape(count, 2, WIN, 2, WIN, C).transpose(0, 1, 3, 2, 4, 5).reshape(count * 4, WIN, WIN, C)
    both = jnp.concatenate([wins, loc], axis=0)
    return jnp.pad(both, ((0, 0), (0, 1), (0, 1), (0, 0))).astype(F32)


def from_cells(cells, globals_):
    cells = cells.reshape(-1, 8, 8, C)[:, :WIN, :WIN]
    wins = cells[: globals_ * 4].reshape(globals_, 2, 2, WIN, WIN, C)
    return wins.transpose(0, 1, 3, 2, 4, 5).reshape(globals_, SIDE, SIDE, C), cells[globals_ * 4 :]


def cell_mask(extent, globals_):
    places = jnp.arange(8, dtype=jnp.int32)
    size = jnp.concatenate([jnp.full((globals_ * 4, 2), WIN, jnp.int32), extent.astype(jnp.int32)], axis=0)
    rows = places[None, :, None] < size[:, 0][:, None, None]
    cols = places[None, None, :] < size[:, 1][:, None, None]
    return jnp.logical_and(rows, cols).astype(F32)


def layer(sizes, tokens, cotangent, mask4, small, w_att, w_ffn):
    windows = 4 * sizes[0] + sizes[1]
    rows = windows * CELL
    mask = jnp.broadcast_to(mask4.reshape(rows, 1), (rows, LANES))
    u = (tokens * mask4[..., None]).reshape(windows * 8, 8, C)
    dy = cotangent.reshape(rows, C)
    kept = []
    for b in range(2):
        r, *att = attention_forward(sizes, b, u, mask, small[b], w_att[b])
        x, *ffn = ffn_forward(sizes, r, mask, small[b], w_ffn[b])
        kept.append((u, r, att, ffn))
        u = x.reshape(windows * 8, 8, C)
    out = u
    grads = []
    for b in (1, 0):
        u, r, att, ffn = kept[b]
        dr, dw_ffn, ds_ffn = ffn_backward(sizes, dy, r, *ffn, mask, small[b], w_ffn[b])
        du, dw_att, ds_att = attention_backward(sizes, b, dr, u, *att, mask, small[b], w_att[b])
        dy = du.reshape(rows, C)
        table = jnp.concatenate(
            [ds_att[0:10], ds_att[13:14], ds_att[10:12], ds_att[14:15], ds_ffn[1:3], ds_att[12:13], ds_ffn[0:1], ds_ffn[3:7]]
        )
        grads.append((dw_att, dw_ffn, table))
    return out, du * mask4.reshape(windows * 8, 8, 1), grads[::-1]


def body(
    global_tokens,
    local_tokens,
    crop_extent,
    conv_weight,
    vectors,
    gains,
    qkv_weight,
    proj_weight,
    fc1_weight,
    fc1_bias,
    fc2_weight,
    global_cotangent,
    local_cotangent,
):
    shards = lax.axis_size("fsdp")
    part = C // shards
    globals_, locals_ = global_tokens.shape[0], local_tokens.shape[0]
    sizes = (globals_, locals_, shards)

    own_small = jnp.concatenate([conv_weight, vectors, gains], axis=1)
    small = lax.all_gather(own_small, "fsdp", axis=2, tiled=True)
    bias = lax.all_gather(fc1_bias, "fsdp", axis=1, tiled=True).reshape(2, FF // C, C)
    small = jnp.concatenate([small, bias], axis=1).astype(F32)
    small = jnp.pad(small, ((0, 0), (0, 2), (0, 0)))
    w_att, w_ffn = [], []
    for b in range(2):
        cols = lambda w, n: [w[b][:, i * C : (i + 1) * C] for i in range(n)]
        packed = jnp.concatenate(
            cols(qkv_weight, 3) + [proj_weight[b]] + cols(fc1_weight, 4) + [fc2_weight[b]], axis=0
        )
        whole = lax.all_gather(packed, "fsdp", axis=0)
        w_att.append(whole[:, : 4 * part])
        w_ffn.append(whole[:, 4 * part :])

    mask4 = cell_mask(crop_extent, globals_)
    out, grad, grads = layer(
        sizes,
        to_cells(global_tokens, local_tokens),
        to_cells(global_cotangent, local_cotangent),
        mask4, small, w_att, w_ffn,
    )
    out = from_cells(out.astype(BF), globals_)
    grad = from_cells(grad, globals_)
    final = []
    for b in range(2):
        dw_att, dw_ffn, _ = grads[b]
        both = jnp.concatenate([dw_att, dw_ffn], axis=1)
        own = lax.psum_scatter(both, "fsdp", scatter_dimension=0, tiled=True)[0]
        final.append(lax.psum(own, "dp").astype(F32))
    table = jnp.stack([grads[0][2], grads[1][2]]).astype(BF)
    main = lax.psum_scatter(table[:, :18], "fsdp", scatter_dimension=2, tiled=True)
    bias = lax.psum_scatter(table[:, 18:].reshape(2, FF), "fsdp", scatter_dimension=1, tiled=True)
    main = lax.psum(main, "dp").astype(F32)
    bias = lax.psum(bias, "dp").astype(F32)

    def cut(start, n, width):
        rows = width
        return jnp.stack(
            [jnp.concatenate([w[(start + i) * rows : (start + i + 1) * rows] for i in range(n)], axis=1) for w in final]
        )

    fc2 = jnp.stack([w[8 * part :] for w in final])
    return (
        out[0], out[1], grad[0], grad[1],
        main[:, 0:9], main[:, 9:16], main[:, 16:18],
        cut(0, 3, part), cut(3, 1, part), cut(4, 4, part), bias, fc2,
    )


def solution(mesh):
    crops = P(("dp", "fsdp"), None, None, None)
    last = P(None, None, "fsdp")
    middle = P(None, "fsdp", None)
    return jax.shard_map(
        body,
        mesh=mesh,
        in_specs=(
            crops, crops, P(("dp", "fsdp"), None), last, last, last, middle, middle, middle,
            P(None, "fsdp"), middle, crops, crops,
        ),
        out_specs=(
            crops, crops, crops, crops, last, last, last, middle, middle, middle, P(None, "fsdp"), middle,
        ),
        check_vma=False,
    )
```

time: 1080 us -> 599 us (0.55)
  local copies, waits for them, and re-layouts: 381 us -> 35.7 us
  Pallas kernels: 0 us -> 242 us
  matrix products: 202 us -> 0 us
  other arithmetic: 145 us -> 23.1 us
  waiting for transfers between devices: 262 us -> 238 us
  blocking collectives: 57.3 us -> 40 us
    pallas_call x0 -> x8, Pallas kernels: none -> 242 us  [call(): pl.pallas_call(kernel, out_shape=outs, in_specs=[VMEM] * len(ins), out_sp...]
    dot_general x72 -> x0, matrix products: 202 us -> none  [the longest x48 138 us: contract(): return product(first_operand, second_operand)]
    convert_element_type x42 -> x1, local copies, waits for them, and re-layouts: 130 us -> 0.1 us  [cell_mask(): return jnp.logical_and(rows, cols).astype(F32)]
    unnamed x17 -> x9, waiting for transfers between devices: 132 us -> 68.3 us
    reshape x16 -> x7, local copies, waits for them, and re-layouts: 64.8 us -> 2.78 us  [the longest x2 2.26 us: from_cells(): wins.transpose(0, 1, 3, 2, 4, 5).reshape(globals_, SIDE, SIDE, C)]
    all_gather x4 -> x2, waiting for transfers between devices: 0.07 us -> 61.9 us  [body(): whole = lax.all_gather(packed, 'fsdp', axis=0)]
    reduce_sum x38 -> x0, other arithmetic: 60.7 us -> none  [the longest x5 13.3 us: softmax_rows(): shifted = scores - jnp.max(scores, axis=-1, keepdims=True)]
    slice x10 -> x24, local copies, waits for them, and re-layouts: 77.4 us -> 19.2 us  [the longest x2 8.93 us: body(): w_ffn.append(whole[:, 4 * part:])]
  transfers between devices with their start and end apart: 13 -> 7, of which waited for: 7 -> 6; matrix products, arithmetic and copies ran while one was open for 33% -> 5% of each run, Pallas kernels for 0% -> 13%
where the time goes in v1:
time: 599 us; the launch traced here: 595 us
  Pallas kernels  242 us (40%)
  waiting for transfers between devices  238 us (40%)
  blocking collectives  40 us (7%)
  local copies, waits for them, and re-layouts  35.7 us (6%)
  other arithmetic  23.1 us (4%)
  between operations  15 us (3%)
    pallas_call x8, Pallas kernels, call(): pl.pallas_call(kernel, out_shape=outs, in_specs=[VMEM] * len(ins), out_sp...  242 us
    unnamed x9, waiting for transfers between devices  68.3 us
    all_gather x2, waiting for transfers between devices, body(): whole = lax.all_gather(packed, 'fsdp', axis=0)  61.9 us
    reduce_scatter x2, waiting for transfers between devices, body(): own = lax.psum_scatter(both, 'fsdp', scatter_dimension=0, tiled=True)[0]  58.3 us
    psum x1, waiting for transfers between devices, body(): final.append(lax.psum(own, 'dp').astype(F32))  49.5 us
    psum x1, blocking collectives, body(): main = lax.psum(main, 'dp').astype(F32)  19.4 us
  transfers between devices with their start and end apart: 7, of which 6 were waited for; matrix products, arithmetic and copies ran while one was open for 5% of the time, Pallas kernels for 13%

profile of v1, /device:TPU:0, one launch (start us, length us, event | category | flops | bytes accessed | tf_op | source)
XLA Modules:
  0.0 594.6 jit_solution(16210611988046906285)
XLA Ops:
  13.0 10.3 %all_gather.19 = bf16[2,2048]{1,0:T(2,128)(2,1)S(1)} all-gather(bf16[2,256]{1,0:T(2,128)(2,1)S(1)} %copy-done.16), channel_id=1, replica_groups=mesh['dp'=4,'fsdp'=8] {'fsdp'}, dimensions={1}, use_global_device_ids=true | all-gather | bytes 9216 | tf_op jit(solution)/shard_map/all_gather | solution.py:618
  23.9 10.3 %all_gather.18 = bf16[2,18,512]{1,0,2:T(2,128)(2,1)S(1)} all-gather(bf16[2,18,64]{1,0,2:T(2,128)(2,1)S(1)} %pad_maximum_fusion.6), channel_id=1, replica_groups=mesh['dp'=4,'fsdp'=8] {'fsdp'}, dimensions={2}, use_global_device_ids=true | all-gather | bytes 41472 | tf_op jit(solution)/shard_map/all_gather | solution.py:617
  37.6 2.0 bitcast_convert_fusion.dy_ref
  39.6 21.4 %all-gather.5.cloned.1.call-done = bf16[6144,512]{1,0:T(8,128)(2,1)} async-done(((bf16[768,512]{1,0:T(8,128)(2,1)}), bf16[6144,512]{1,0:T(8,128)(2,1)}) %all-gather.5.cloned.1.call-update) | async-done | bytes 6291472 | tf_op jit(solution)/shard_map/all_gather | solution.py:627
  61.0 3.1 slice.341.w_ref
  64.1 4.4 slice.342.w_ref
  68.5 40.5 %all-gather.7.cloned.1.call-done = bf16[6144,512]{1,0:T(8,128)(2,1)} async-done(((bf16[768,512]{1,0:T(8,128)(2,1)}), bf16[6144,512]{1,0:T(8,128)(2,1)}) %all-gather.7.cloned.1.call-update) | async-done | bytes 6291472 | tf_op jit(solution)/shard_map/all_gather | solution.py:627
  109.0 3.0 slice.351.w_ref
  112.1 4.5 slice.352.w_ref
  117.7 33.4 %shard_map.220 = (f32[1344,512]{1,0:T(8,128)}, f32[168,8,512]{2,1,0:T(8,128)}, bf16[1344,512]{1,0:T(8,128)(2,1)}, bf16[1344,512]{1,0:T(8,128)(2,1)}, bf16[1344,5...) custom-call(f32[168,8,512]{2,1,0:T(8,128)} %bitcast.78, ...), custom_call_target="tpu_custom_call" | custom-call | tf_op jit(solution)/shard_map/pallas_call | solution.py:42
  151.1 21.5 %shard_map.221 = (f32[1344,512]{1,0:T(8,128)}, bf16[1344,512]{1,0:T(8,128)(2,1)}, bf16[1344,2048]{1,0:T(8,128)(2,1)}, bf16[1344,2048]{1,0:T(8,128)(2,1)}) custom-call(f32[1344,512]{1,0:T(8,128)} %get-tuple-element.48.r_ref, f32[1344,128]{1,0:T(8,128)} %broadcast_in_dim.2.mask_ref, f32[24,512]{1,0:T(8,128)} %get-tuple-element.183.small_ref, ...), custom_call_target="tpu_custom_call" | custom-call | tf_op jit(solution)/shard_map/pallas_call | solution.py:42
  172.6 22.8 %shard_map.222 = (f32[1344,512]{1,0:T(8,128)}, f32[168,8,512]{2,1,0:T(8,128)}, bf16[1344,512]{1,0:T(8,128)(2,1)}, bf16[1344,512]{1,0:T(8,128)(2,1)}, bf16[1344,5...) custom-call(f32[168,8,512]{2,1,0:T(8,128)} %bitcast.80, ...), custom_call_target="tpu_custom_call" | custom-call | tf_op jit(solution)/shard_map/pallas_call | solution.py:42
  195.4 21.9 %shard_map.223 = (f32[1344,512]{1,0:T(8,128)}, bf16[1344,512]{1,0:T(8,128)(2,1)}, bf16[1344,2048]{1,0:T(8,128)(2,1)}, bf16[1344,2048]{1,0:T(8,128)(2,1)}) custom-call(f32[1344,512]{1,0:T(8,128)} %get-tuple-element.50.r_ref, f32[1344,128]{1,0:T(8,128)} %broadcast_in_dim.2.mask_ref, f32[24,512]{1,0:T(8,128)} %get-tuple-element.182.small_ref, ...), custom_call_target="tpu_custom_call" | custom-call | tf_op jit(solution)/shard_map/pallas_call | solution.py:42
  217.4 29.0 %shard_map.224 = (f32[1344,512]{1,0:T(8,128)}, bf16[8,512,512]{2,1,0:T(8,128)(2,1)}, f32[8,512]{1,0:T(8,128)}) custom-call(f32[1344,512]{1,0:T(8,128)} %bitcast_convert_fusion.dy_ref, f32[1344,512]{1,0:T(8,128)} %get-tuple-element.50.r_ref, bf16[1344,512]{1,0:T(8,128)(2,1)} %get-tuple-element.52.n_ref, bf16[1344,2048]{1,0:T(8,128)(2,1)} %get-tuple-element.53.g_ref, ...), custom_call_target="tpu_custom_call" | custom-call | tf_op jit(solution)/shard_map/pallas_call | solution.py:42
  246.3 37.2 %shard_map.225 = (f32[168,8,512]{2,1,0:T(8,128)}, bf16[8,256,512]{2,1,0:T(8,128)(2,1)}, f32[16,512]{1,0:T(8,128)}) custom-call(f32[1344,512]{1,0:T(8,128)} %get-tuple-element.55.dr_ref, f32[168,8,512]{2,1,0:T(8,128)} %bitcast.81, f32[168,8,512]{2,1,0:T(8,128)} %get-tuple-element.56.c_ref, bf16[1344,512]{1,0:T(8,128)(2,1)} %get-tuple-element.57.n_ref, ...), custom_call_target="tpu_custom_call" | custom-call | tf_op jit(solution)/shard_map/pallas_call | solution.py:42
  283.6 5.8 pad_maximum_fusion.1
  289.5 29.8 %shard_map.226 = (f32[1344,512]{1,0:T(8,128)}, bf16[8,512,512]{2,1,0:T(8,128)(2,1)}, f32[8,512]{1,0:T(8,128)}) custom-call(f32[1344,512]{1,0:T(8,128)} %bitcast.92, f32[1344,512]{1,0:T(8,128)} %get-tuple-element.48.r_ref, bf16[1344,512]{1,0:T(8,128)(2,1)} %get-tuple-element.64.n_ref, bf16[1344,2048]{1,0:T(8,128)(2,1)} %get-tuple-element.65.g_ref, ...), custom_call_target="tpu_custom_call" | custom-call | tf_op jit(solution)/shard_map/pallas_call | solution.py:42
  319.3 46.7 %shard_map.227 = (f32[168,8,512]{2,1,0:T(8,128)}, bf16[8,256,512]{2,1,0:T(8,128)(2,1)}, f32[16,512]{1,0:T(8,128)}) custom-call(f32[1344,512]{1,0:T(8,128)} %get-tuple-element.67.dr_ref, f32[168,8,512]{2,1,0:T(8,128)} %bitcast.79, f32[168,8,512]{2,1,0:T(8,128)} %get-tuple-element.68.c_ref, bf16[1344,512]{1,0:T(8,128)(2,1)} %get-tuple-element.69.n_ref, ...), custom_call_target="tpu_custom_call" | custom-call | tf_op jit(solution)/shard_map/pallas_call | solution.py:42
  366.0 6.0 %pad_maximum_fusion = bf16[8,768,512]{2,1,0:T(8,128)(2,1)} fusion(bf16[8,512,512]{2,1,0:T(8,128)(2,1)} %get-tuple-element.81, bf16[8,256,512]{2,1,0:T(8,128)(2,1)} %get-tuple-element.80), kind=kLoop, calls=%fused_computation | loop fusion | flops 12582912 | bytes 12582912 | tf_op jit(solution)/shard_map/concatenate | solution.py:643
  375.5 58.3 %reduce-scatter.9.cloned.1.call-done = bf16[1,768,512]{2,1,0:T(8,128)(2,1)} async-done(((bf16[8,768,512]{2,1,0:T(8,128)(2,1)}), bf16[1,768,512]{2,1,0:T(8,128)(2,1)}) %reduce-scatter.9.cloned.1.call-update) | async-done | bytes 786448 | tf_op jit(solution)/shard_map/reduce_scatter | solution.py:644
  439.9 31.5 %reduce-scatter.15.cloned.1.call-done = bf16[256,2]{1,0:T(8,128)(2,1)} async-done(((bf16[2048,2]{1,0:T(8,128)(2,1)}), bf16[256,2]{1,0:T(8,128)(2,1)}) %reduce-scatter.15.cloned.1.call-update) | async-done | bytes 1040
  472.3 36.2 %reduce-scatter.13.cloned.1.call-done = bf16[64,36]{1,0:T(8,128)(2,1)} async-done(((bf16[512,36]{1,0:T(8,128)(2,1)}), bf16[64,36]{1,0:T(8,128)(2,1)}) %reduce-scatter.13.cloned.1.call-update) | async-done | bytes 4624
  509.4 19.4 %all-reduce.4 = (bf16[2,18,64]{2,1,0:T(8,128)(2,1)S(1)}, bf16[2,256]{1,0:T(2,128)(2,1)S(1)}) all-reduce(bf16[2,18,64]{2,1,0:T(8,128)(2,1)S(1)} %copy.77, bf16[2,256]{1,0:T(2,128)(2,1)S(1)} %copy.79), channel_id=1, replica_groups=mesh['dp'=4,'fsdp'=8] {'dp'}, use_global_device_ids=true, to_apply=%region_1.2 | all-reduce | flops 2816 | bytes 11264 | tf_op jit(solution)/shard_map/psum | solution.py:649
  531.1 49.5 %all-reduce.8.cloned.1.call-done = (bf16[768,512]{1,0:T(8,128)(2,1)}, bf16[768,512]{1,0:T(8,128)(2,1)}) async-done(((bf16[768,512]{1,0:T(8,128)(2,1)}, bf16[768,512]{1,0:T(8,128)(2,1)}), (bf16[768,512]{1,0:T(8,128)(2,1)}, bf16[768,512]{1,0:T(8,128)(2,1)})) %all-reduce.8.cloned.1.call-update) | async-done | bytes 1572880 | tf_op jit(solution)/shard_map/psum | solution.py:645
  (147 shorter events, 31.0 us)
Async XLA Ops:
  7.2 3.4 copy-start.7
  7.2 53.8 %all-gather.5.cloned.1.call-start = ((), (), s32[]{:S(2)}) async-start(), calls=%async_computation.6 | async-start | bytes 7077888 | tf_op jit(solution)/shard_map/all_gather | solution.py:627
  8.4 4.0 copy-start.5
  10.5 2.1 copy-start.18
  10.6 2.4 copy-start.16
  10.6 12.8 %copy-start.17 = (bf16[2,2,64]{2,1,0:T(2,128)(2,1)S(1)}, bf16[2,2,64]{2,1,0:T(2,128)(2,1)}, u32[]{:S(2)}) copy-start(bf16[2,2,64]{2,1,0:T(2,128)(2,1)} %param.18) | copy-start | bytes 1540
  10.6 12.9 %copy-start.15 = (bf16[2,7,64]{2,0,1:T(2,128)(2,1)S(1)}, bf16[2,7,64]{2,0,1:T(2,128)(2,1)}, u32[]{:S(2)}) copy-start(bf16[2,7,64]{2,0,1:T(2,128)(2,1)} %param.17) | copy-start | bytes 5380
  10.6 13.0 %copy-start.14 = (bf16[2,9,64]{2,0,1:T(2,128)(2,1)S(1)}, bf16[2,9,64]{2,0,1:T(2,128)(2,1)}, u32[]{:S(2)}) copy-start(bf16[2,9,64]{2,0,1:T(2,128)(2,1)} %param.16) | copy-start | bytes 6916
  10.7 0.9 copy-start.4
  10.7 1.1 copy-start.3
  10.7 23.7 %copy-start.6 = (bf16[3,14,14,512]{3,2,1,0:T(8,128)(2,1)S(1)}, bf16[3,14,14,512]{3,2,1,0:T(8,128)(2,1)}, u32[]{:S(2)}) copy-start(bf16[3,14,14,512]{3,2,1,0:T(8,128)(2,1)} %param.24) | copy-start | bytes 1806340
  11.6 97.4 %all-gather.7.cloned.1.call-start = ((), (), s32[]{:S(2)}) async-start(), calls=%async_computation.7 | async-start | bytes 7077888 | tf_op jit(solution)/shard_map/all_gather | solution.py:627
  12.3 363.1 %reduce-scatter.11.cloned.1.call-start = ((), (), s32[]{:S(2)}) async-start(), calls=%async_computation.5 | async-start | bytes 7077888 | tf_op jit(solution)/shard_map/reduce_scatter | solution.py:644
  12.5 22.7 %copy-start.8 = (bf16[9,7,7,512]{3,2,1,0:T(8,128)(2,1)S(1)}, bf16[9,7,7,512]{3,2,1,0:T(8,128)(2,1)}, u32[]{:S(2)}) copy-start(bf16[9,7,7,512]{3,2,1,0:T(8,128)(2,1)} %param.25) | copy-start | bytes 1354756
  34.4 1.3 copy-start.9
  289.4 144.3 %reduce-scatter.9.cloned.1.call-start = ((), (), s32[]{:S(2)}) async-start(), calls=%async_computation.4 | async-start | bytes 7077888 | tf_op jit(solution)/shard_map/reduce_scatter | solution.py:644
  372.0 0.8 copy-start.10
  372.0 0.8 copy-start.11
  372.0 61.9 %copy-start.2 = (f32[1344,512]{1,0:T(8,128)S(1)}, f32[1344,512]{1,0:T(8,128)}, u32[]{:S(2)}) copy-start(f32[1344,512]{1,0:T(8,128)} %get-tuple-element.51) | copy-start | bytes 8257540
  372.0 99.3 %reduce-scatter.15.cloned.1.call-start = ((), (), s32[]{:S(2)}) async-start(), calls=%async_computation.9 | async-start | bytes 589824
  374.1 134.3 %reduce-scatter.13.cloned.1.call-start = ((), (), s32[]{:S(2)}) async-start(), calls=%async_computation.8 | async-start | bytes 147456
  375.2 205.4 %all-reduce.8.cloned.1.call-start = ((), (), s32[]{:S(2)}) async-start(), calls=%async_computation.10 | async-start | bytes 3145728 | tf_op jit(solution)/shard_map/psum | solution.py:645
  434.0 2.0 copy-start.1
  580.6 2.6 copy-start
  (2 other events, 1.5 us)
Sparse Core Ops, SparseCore 0:
  11.7 49.2 all-gather.4
  63.5 45.5 all-gather.6
  289.6 61.8 reduce-scatter.10
  372.2 61.5 reduce-scatter.8
  437.2 34.0 reduce-scatter.14
  475.1 33.3 reduce-scatter.12
  510.9 69.6 all-reduce.7

commit v2 on v1

v2 whole, which is shorter than its diff:
```python
import functools

import jax
import jax.numpy as jnp
from jax import lax
from jax.experimental import pallas as pl
from jax.experimental.pallas import tpu as pltpu
from jax.sharding import PartitionSpec as P

BF = jnp.bfloat16
F32 = jnp.float32
C = 512
FF = 2048
HEAD = 32
WIN = 7
SIDE = 14
CELL = 64
LANES = 128
GROUPS = C // LANES
PER = LANES // HEAD
EPS = 1e-5
SCALE = HEAD ** -0.5
MIX_UNROLL = 7
NORM_UNROLL = 7
VMEM = pl.BlockSpec(memory_space=pltpu.VMEM)
HELD = pl.BlockSpec(memory_space=pl.ANY)
NT = (((1,), (1,)), ((), ()))
TN = (((0,), (0,)), ((), ()))
K_ROW, V_ROW, G_ROW, B_ROW, TAB = 0, 9, 16, 18, 32


def mm(a, b):
    return jnp.dot(a, b, preferred_element_type=F32)


def mm_nt(a, b):
    return lax.dot_general(a, b, NT, preferred_element_type=F32)


def mm_tn(a, b):
    return lax.dot_general(a, b, TN, preferred_element_type=F32)


class Copy:
    def __init__(self, src, dst, sems, ref):
        self.src, self.dst, self.sems, self.ref = src, dst, sems, ref
        self.open = {}

    def start(self, k=0, part=None):
        src, dst = (self.src, self.dst) if part is None else (self.src.at[part], self.dst.at[part])
        self.open[k] = pltpu.make_async_copy(src, dst, self.sems.at[k])
        self.open[k].start()

    def wait(self, k=0):
        self.open.pop(k).wait()
        return self.ref

    def wait_all(self):
        for k in list(self.open):
            self.wait(k)


PARTS = 4


def call(kernel, me, ins, outs, held=(), packs=(), scratch=(), flops=0, limit=62):
    n_in, n_out, n_held, n_pack = len(ins), len(outs), len(held), len(packs)

    def body(me_ref, *refs):
        src, refs = refs[:n_in], refs[n_in:]
        held_refs, refs = refs[:n_held], refs[n_held:]
        dst, refs = refs[:n_out], refs[n_out:]
        pack_refs, refs = refs[:n_pack], refs[n_pack:]
        in_vmem, refs = refs[:n_in], refs[n_in:]
        out_vmem, refs = refs[:n_out], refs[n_out:]
        in_sem, out_sem, refs = refs[0], refs[1], refs[2:]
        feeds = [Copy(s, v, in_sem.at[i], v) for i, (s, v) in enumerate(zip(src, in_vmem))]
        sends = [Copy(v, d, out_sem.at[i], v) for i, (d, v) in enumerate(zip(dst, out_vmem))]
        kernel(me_ref, feeds, sends, held_refs, pack_refs, *refs)
        for send in sends:
            send.wait_all()

    vmem = lambda v: pltpu.VMEM(v.shape, v.dtype)
    return pl.pallas_call(
        body,
        out_shape=list(outs) + list(packs),
        in_specs=[pl.BlockSpec(memory_space=pltpu.SMEM)] + [HELD] * (n_in + n_held),
        out_specs=[HELD] * (n_out + n_pack),
        scratch_shapes=[vmem(v) for v in ins]
        + [vmem(v) for v in outs]
        + [pltpu.SemaphoreType.DMA((max(n_in, 1), PARTS)), pltpu.SemaphoreType.DMA((max(n_out, 1), PARTS))]
        + list(scratch),
        compiler_params=pltpu.CompilerParams(vmem_limit_bytes=limit * 2**20),
        cost_estimate=pl.CostEstimate(flops=flops, bytes_accessed=20 * 2**20, transcendentals=0),
    )(me, *ins, *held)


def start_weights(bufs, me_ref, plan, sem):
    copies = []
    if len(bufs) == 1:
        sources = [(d, bufs[0].at[d]) for d in range(bufs[0].shape[0])]
    else:
        sources = [(me_ref[0] ^ k, buf) for k, buf in enumerate(bufs)]
    for d, src in sources:
        for first, rows, place in plan:
            copies.append(pltpu.make_async_copy(src.at[pl.ds(first, rows), :], place(d), sem))
    for copy in copies:
        copy.start()
    return copies


def rows_of(ref, i, rows):
    return lambda d: ref.at[i, pl.ds(pl.multiple_of(d * rows, rows), rows), :]


def slot_of(d, me_ref, relative):
    if not relative:
        return d
    turn = me_ref[0] ^ d
    return (turn & 1) * 4 + (turn >> 1)


def shape(dims, kind):
    return jax.ShapeDtypeStruct(dims, kind)


def wide(m):
    return jnp.concatenate([m] * GROUPS, axis=1)


def fold8(v):
    return jnp.sum(v.reshape(v.shape[0] // 8, 8, v.shape[1]), axis=0)


def norm_parts(x):
    center = jnp.sum(x, axis=-1, keepdims=True) * (1.0 / C)
    xc = x - center
    var = jnp.sum(xc * xc, axis=-1, keepdims=True) * (1.0 / C)
    rstd = lax.rsqrt(var + EPS)
    return xc * rstd, rstd


def norm_back(dn, xhat, rstd, gain):
    gp = dn * gain
    m1 = jnp.sum(gp, axis=-1, keepdims=True) * (1.0 / C)
    m2 = jnp.sum(gp * xhat, axis=-1, keepdims=True) * (1.0 / C)
    return rstd * (gp - m1 - xhat * m2)


def several(count, at_once, step):
    while count % at_once:
        at_once -= 1

    @pl.loop(0, count // at_once)
    def _(i):
        for j in range(at_once):
            step(i * at_once + j)


def head_masks(rows):
    lane = lax.broadcasted_iota(jnp.int32, (rows, LANES), 1) // HEAD
    return [lane == h for h in range(PER)]


def spread(v, masks):
    zero = jnp.zeros_like(v)
    return jnp.concatenate([jnp.where(m, v, zero) for m in masks], axis=0)


def gather_heads(full, masks):
    n = full.shape[0] // PER
    out = full[3 * n :]
    for h in (2, 1, 0):
        out = jnp.where(masks[h], full[h * n : (h + 1) * n], out)
    return out


def shifted_cols(left, right, j, step):
    if step == 0:
        return left, right
    if step == 1:
        return (
            jnp.where(j == 6, pltpu.roll(right, 6, 1), pltpu.roll(left, 7, 1)),
            pltpu.roll(right, 7, 1),
        )
    return (
        pltpu.roll(left, 1, 1),
        jnp.where(j == 0, pltpu.roll(left, 2, 1), pltpu.roll(right, 1, 1)),
    )


def canvas(ref, crop, lanes):
    base = crop * 32
    parts = [ref[pl.ds(base + 8 * w, 7), :, lanes] for w in range(4)]
    left = jnp.concatenate([parts[0], parts[2]], axis=0)
    right = jnp.concatenate([parts[1], parts[3]], axis=0)
    return left, right


def put_canvas(ref, crop, lanes, left, right, mask_ref):
    base = crop * 32
    zero = jnp.zeros((1, 8, LANES), F32)
    for w in range(4):
        side = right if w % 2 else left
        half = side[(w // 2) * 7 : (w // 2) * 7 + 7]
        rows = pl.ds(base + 8 * w, 8)
        ref[rows, :, lanes] = jnp.concatenate([half, zero], axis=0) * mask_ref[rows]


def conv_forward(u_ref, c_ref, small_ref, mask_ref, globals_, locals_):
    j14 = lax.broadcasted_iota(jnp.int32, (14, 8, LANES), 1)
    for g in range(GROUPS):
        lanes = pl.ds(g * LANES, LANES)
        taps = [small_ref[K_ROW + t : K_ROW + t + 1, lanes][None] for t in range(9)]
        shift = small_ref[V_ROW : V_ROW + 1, lanes][None]

        @pl.loop(0, globals_)
        def _(crop):
            left, right = canvas(u_ref, crop, lanes)
            zero = jnp.zeros((1, 8, LANES), F32)
            acc = [left + shift, right + shift]
            for e in (-1, 0, 1):
                for s, side in enumerate(shifted_cols(left, right, j14, e)):
                    tall = jnp.concatenate([zero, side, zero], axis=0)
                    for a in (-1, 0, 1):
                        acc[s] = acc[s] + taps[3 * (a + 1) + e + 1] * tall[1 + a : 15 + a]
            put_canvas(c_ref, crop, lanes, acc[0], acc[1], mask_ref)

        @pl.loop(0, locals_)
        def _(n):
            rows = pl.ds(globals_ * 32 + n * 8, 8)
            u = u_ref[rows, :, lanes]
            acc = u + shift
            for e in (-1, 0, 1):
                side = u if e == 0 else pltpu.roll(u, 7 if e == 1 else 1, 1)
                for a in (-1, 0, 1):
                    moved = side if a == 0 else jnp.roll(side, -a, axis=0)
                    acc = acc + taps[3 * (a + 1) + e + 1] * moved
            c_ref[rows, :, lanes] = acc * mask_ref[rows]


def conv_backward(d_ref, u_ref, du_ref, small_ref, acc_ref, globals_, locals_):
    j14 = lax.broadcasted_iota(jnp.int32, (14, 8, LANES), 1)
    for g in range(GROUPS):
        lanes = pl.ds(g * LANES, LANES)
        taps = [small_ref[K_ROW + t : K_ROW + t + 1, lanes][None] for t in range(9)]
        nothing = tuple(jnp.zeros((8, LANES), F32) for _ in range(10))

        def one_crop(crop, sums):
            sums = list(sums)
            left, right = canvas(d_ref, crop, lanes)
            own = canvas(u_ref, crop, lanes)
            zero = jnp.zeros((1, 8, LANES), F32)
            acc = [left, right]
            sums[9] = sums[9] + jnp.sum(left + right, axis=0)
            for e in (-1, 0, 1):
                for s, side in enumerate(shifted_cols(left, right, j14, -e)):
                    tall = jnp.concatenate([zero, side, zero], axis=0)
                    for a in (-1, 0, 1):
                        t = 3 * (a + 1) + e + 1
                        moved = tall[1 - a : 15 - a]
                        acc[s] = acc[s] + taps[t] * moved
                        sums[t] = sums[t] + jnp.sum(own[s] * moved, axis=0)
            base = crop * 32
            for w in range(4):
                side = acc[w % 2]
                half = side[(w // 2) * 7 : (w // 2) * 7 + 7]
                du_ref[pl.ds(base + 8 * w, 8), :, lanes] = jnp.concatenate([half, zero], axis=0)
            return tuple(sums)

        def one_local(n, sums):
            sums = list(sums)
            rows = pl.ds(globals_ * 32 + n * 8, 8)
            d = d_ref[rows, :, lanes]
            own = u_ref[rows, :, lanes]
            acc = d
            sums[9] = sums[9] + jnp.sum(d, axis=0)
            for e in (-1, 0, 1):
                side = d if e == 0 else pltpu.roll(d, 7 if e == -1 else 1, 1)
                for a in (-1, 0, 1):
                    t = 3 * (a + 1) + e + 1
                    moved = side if a == 0 else jnp.roll(side, a, axis=0)
                    acc = acc + taps[t] * moved
                    sums[t] = sums[t] + jnp.sum(own * moved, axis=0)
            du_ref[rows, :, lanes] = acc
            return tuple(sums)

        sums = lax.fori_loop(0, globals_, one_crop, nothing)
        sums = lax.fori_loop(0, locals_, one_local, sums)
        for t in range(10):
            acc_ref[t, :, lanes] = sums[t]


def spatial_forward(q_ref, k_ref, v_ref, mask_ref, o_ref, p_ref, windows):
    masks = head_masks(CELL)

    def step(w):
        rows = pl.ds(w * CELL, CELL)
        m = mask_ref[rows, :]
        valid = jnp.concatenate([m, m], axis=1) > 0.5
        for g in range(GROUPS):
            lanes = pl.ds(g * LANES, LANES)
            s = mm_nt(k_ref[rows, lanes], spread(q_ref[rows, lanes], masks))
            s = jnp.where(valid, s * SCALE, -1e9)
            e = jnp.exp(s - jnp.max(s, axis=0, keepdims=True))
            p = (e / jnp.sum(e, axis=0, keepdims=True)).astype(BF)
            p_ref[w, g] = p
            o_ref[rows, lanes] = gather_heads(mm_tn(p, v_ref[rows, lanes]), masks).astype(BF)

    several(windows, MIX_UNROLL, step)


def plus(a, b):
    return b if a is None else a + b


def pick(count, at_once):
    while count % at_once:
        at_once -= 1
    return at_once


def spatial_backward(q_ref, k_ref, v_ref, p_ref, do_ref, dq_ref, dk_ref, dv_ref, acc_ref, s_ref, windows, wait, send):
    masks = head_masks(CELL)
    lanes = [pl.ds(g * LANES, LANES) for g in range(GROUPS)]
    at_once = pick(windows, MIX_UNROLL)
    for ready in wait:
        ready()

    @pl.loop(0, windows // at_once)
    def _(i):
        sums = [None] * GROUPS
        for w in [i * at_once + j for j in range(at_once)]:
            rows = pl.ds(w * CELL, CELL)
            for g in range(GROUPS):
                p = p_ref[w, g]
                dos = spread(do_ref[rows, lanes[g]], masks)
                dp = mm_nt(v_ref[rows, lanes[g]], dos)
                pf = p.astype(F32)
                total = jnp.sum(pf * dp, axis=0, keepdims=True)
                ds = (pf * (dp - total) * SCALE).astype(BF)
                s_ref[w, g] = ds
                dv = mm(p, dos)
                sums[g] = plus(sums[g], fold8(dv))
                dv_ref[rows, lanes[g]] = dv.astype(BF)
                dk_ref[rows, lanes[g]] = mm(ds, spread(q_ref[rows, lanes[g]], masks)).astype(BF)
        for g in range(GROUPS):
            acc_ref[1, :, lanes[g]] += sums[g]

    send[1]()
    send[2]()

    @pl.loop(0, windows // at_once)
    def _(i):
        sums = [None] * GROUPS
        for w in [i * at_once + j for j in range(at_once)]:
            rows = pl.ds(w * CELL, CELL)
            for g in range(GROUPS):
                dq = gather_heads(mm_tn(s_ref[w, g], k_ref[rows, lanes[g]]), masks)
                sums[g] = plus(sums[g], fold8(dq))
                dq_ref[rows, lanes[g]] = dq.astype(BF)
        for g in range(GROUPS):
            acc_ref[0, :, lanes[g]] += sums[g]

    send[0]()


def same_head():
    a = lax.broadcasted_iota(jnp.int32, (LANES, LANES), 0) // HEAD
    b = lax.broadcasted_iota(jnp.int32, (LANES, LANES), 1) // HEAD
    return a == b


def over_crops(globals_, locals_, step):
    several(globals_, 3, lambda n: step(n, n * 4 * CELL, 4 * CELL))
    several(locals_, 9, lambda n: step(globals_ + n, globals_ * 4 * CELL + n * CELL, CELL))


def channel_forward(q_ref, k_ref, v_ref, mask_ref, o_ref, p_ref, globals_, locals_):
    same = same_head()
    lanes = [pl.ds(g * LANES, LANES) for g in range(GROUPS)]

    def weigh(n, start, count):
        rows = pl.ds(start, count)
        m = mask_ref[rows, :].astype(BF)
        for g in range(GROUPS):
            s = mm_tn(v_ref[rows, lanes[g]], k_ref[rows, lanes[g]] * m)
            s = jnp.where(same, s * SCALE, -jnp.inf)
            e = jnp.exp(s - jnp.max(s, axis=0, keepdims=True))
            p_ref[n, g] = (e / jnp.sum(e, axis=0, keepdims=True)).astype(BF)

    over_crops(globals_, locals_, weigh)

    def step(n, start, count):
        rows = pl.ds(start, count)
        for g in range(GROUPS):
            o_ref[rows, lanes[g]] = mm(q_ref[rows, lanes[g]], p_ref[n, g]).astype(BF)

    over_crops(globals_, locals_, step)


def channel_backward(
    q_ref, k_ref, v_ref, mask_ref, p_ref, do_ref, dq_ref, dk_ref, dv_ref, acc_ref, s_ref, globals_, locals_, wait, send
):
    lanes = [pl.ds(g * LANES, LANES) for g in range(GROUPS)]

    def slope(n, start, count):
        rows = pl.ds(start, count)
        for g in range(GROUPS):
            dp = mm_tn(q_ref[rows, lanes[g]], do_ref[rows, lanes[g]])
            pf = p_ref[n, g].astype(F32)
            total = jnp.sum(pf * dp, axis=0, keepdims=True)
            s_ref[n, g] = (pf * (dp - total) * SCALE).astype(BF)

    for ready in wait[:3]:
        ready()
    over_crops(globals_, locals_, slope)
    for ready in wait[3:]:
        ready()

    def step(n, start, count):
        rows = pl.ds(start, count)
        mf = mask_ref[rows, :]
        m = mf.astype(BF)
        for g in range(GROUPS):
            ds = s_ref[n, g]
            dq = mm_nt(do_ref[rows, lanes[g]], p_ref[n, g])
            dk = mm(v_ref[rows, lanes[g]], ds) * mf
            dv = mm_nt(k_ref[rows, lanes[g]] * m, ds)
            acc_ref[0, :, lanes[g]] += fold8(dq)
            acc_ref[1, :, lanes[g]] += fold8(dv)
            dq_ref[rows, lanes[g]] = dq.astype(BF)
            dk_ref[rows, lanes[g]] = dk.astype(BF)
            dv_ref[rows, lanes[g]] = dv.astype(BF)

    over_crops(globals_, locals_, step)
    for go in send:
        go()


def table_of(tabs):
    total = tabs[0].astype(F32)
    for d in range(1, tabs.shape[0]):
        total = total + tabs[d].astype(F32)
    return total


CHUNKS = 3


def chunks_of(rows):
    size = rows // CHUNKS
    return [pl.ds(i * size, size) for i in range(CHUNKS)]


def tiles_of(here):
    return pl.ds(here.start // 8, here.size // 8)


def attention_forward(sizes, kind, me, u, mask, bufs, first):
    globals_, locals_, shards = sizes
    windows = 4 * globals_ + locals_
    rows = windows * CELL
    part = C // shards
    chunks = chunks_of(rows)

    def kernel(me_ref, feeds, sends, held, packs, w, tabs, sem, sem2):
        u_in, m_in = feeds
        r_out, small_out, c_out, n_out, q_out, k_out, v_out, o_out, p_out = sends
        r_ref, small_ref, c_ref, n_ref, q_ref, k_ref, v_ref, o_ref, p_ref = [v.ref for v in sends]
        u_in.start()
        tab = start_weights(held, me_ref, [(first + 4 * part, TAB, lambda d: tabs.at[d])], sem2)
        m_in.start()
        plan = [(first + i * part, part, rows_of(w, i, part)) for i in range(4)]
        copies = start_weights(held, me_ref, plan, sem)
        for copy in tab:
            copy.wait()
        small_ref[...] = table_of(tabs)
        small_out.start()
        u_ref = u_in.wait()
        mask_ref = m_in.wait()
        conv_forward(u_ref, c_ref, small_ref, mask_ref.reshape(windows * 8, 8, LANES), globals_, locals_)
        c_out.start()
        gain = small_ref[G_ROW : G_ROW + 1]
        shift = small_ref[V_ROW + 1 : V_ROW + 2]

        def step(i):
            x = c_ref[pl.ds(i * 8, 8)].reshape(CELL, C)
            xhat, _ = norm_parts(x)
            n_ref[pl.ds(i * CELL, CELL), :] = (xhat * gain + shift).astype(BF)

        several(windows, NORM_UNROLL, step)
        n_out.start()
        for copy in copies:
            copy.wait()
        for here in chunks:
            n1 = n_ref[here, :]
            q_ref[here, :] = (mm(n1, w[0]) + small_ref[V_ROW + 2 : V_ROW + 3]).astype(BF)
            k_ref[here, :] = mm(n1, w[1]).astype(BF)
            v_ref[here, :] = (mm(n1, w[2]) + small_ref[V_ROW + 3 : V_ROW + 4]).astype(BF)
        for send in (q_out, k_out, v_out):
            send.start()
        if kind == 0:
            spatial_forward(q_ref, k_ref, v_ref, mask_ref, o_ref, p_ref, windows)
        else:
            channel_forward(q_ref, k_ref, v_ref, mask_ref, o_ref, p_ref, globals_, locals_)
        p_out.start()
        o_out.start()
        for i, here in enumerate(chunks):
            c = c_ref[tiles_of(here)].reshape(here.size, C)
            r_ref[here, :] = c + mm(o_ref[here, :], w[3]) + small_ref[V_ROW + 4 : V_ROW + 5]
            r_out.start(i, here)

    low = shape((rows, C), BF)
    probs = (windows, GROUPS, CELL, PER * CELL) if kind == 0 else (globals_ + locals_, GROUPS, LANES, LANES)
    outs = [
        shape((rows, C), F32), shape((TAB, C), F32), shape((windows * 8, 8, C), F32),
        low, low, low, low, low, shape(probs, BF),
    ]
    scratch = [
        pltpu.VMEM((4, C, C), BF),
        pltpu.VMEM((shards, TAB, C), BF),
        pltpu.SemaphoreType.DMA,
        pltpu.SemaphoreType.DMA,
    ]
    return call(kernel, me, [u, mask], outs, held=bufs, scratch=scratch, flops=12 * rows * C * C)


def ffn_plan(part, deep, w1, w2):
    plan = [(i * part, part, rows_of(w1, i, part)) for i in range(FF // C)]
    return plan + [((FF // C) * part, deep, lambda d: w2.at[pl.ds(pl.multiple_of(d * deep, deep), deep), :])]


def ffn_forward(sizes, me, r, mask, small, bufs):
    globals_, locals_, shards = sizes
    windows = 4 * globals_ + locals_
    rows = windows * CELL
    part = C // shards
    deep = FF // shards
    chunks = chunks_of(rows)

    def kernel(me_ref, feeds, sends, held, packs, w1, w2, sem):
        r_in, m_in, small_in = feeds
        x_out, n_out, g_out, s_out = sends
        x_ref, n_ref, g_ref, s_ref = [v.ref for v in sends]
        small_in.start()
        r_in.start()
        copies = start_weights(held, me_ref, ffn_plan(part, deep, w1, w2), sem)
        m_in.start()
        small_ref = small_in.wait()
        gain = small_ref[G_ROW + 1 : G_ROW + 2]
        shift = small_ref[V_ROW + 5 : V_ROW + 6]
        r_ref = r_in.wait()

        def step(i):
            here = pl.ds(i * CELL, CELL)
            xhat, _ = norm_parts(r_ref[here, :])
            n_ref[here, :] = (xhat * gain + shift).astype(BF)

        several(windows, NORM_UNROLL, step)
        n_out.start()
        mask_ref = m_in.wait()
        for copy in copies:
            copy.wait()
        for i, here in enumerate(chunks):
            n2 = n_ref[here, :]
            for t in range(FF // C):
                h = mm(n2, w1[t]) + small_ref[B_ROW + t : B_ROW + t + 1]
                h2 = h * h
                a = 0.5 + 0.5 * jnp.tanh(h * (0.7978845608 + (0.7978845608 * 0.044715) * h2))
                g = h * a
                slope = a + (2.0 * g) * (1.0 - a) * (0.7978845608 + (3 * 0.7978845608 * 0.044715) * h2)
                g_ref[here, t * C : (t + 1) * C] = g.astype(BF)
                s_ref[here, t * C : (t + 1) * C] = slope.astype(BF)
            g_out.start(i, here)
            s_out.start(i, here)
            y = r_ref[here, :] + mm(g_ref[here, :], w2[...]) + small_ref[V_ROW + 6 : V_ROW + 7]
            x_ref[here, :] = y * wide(mask_ref[here, :])
            x_out.start(i, here)

    high = shape((rows, FF), BF)
    outs = [shape((rows, C), F32), shape((rows, C), BF), high, high]
    scratch = [pltpu.VMEM((FF // C, C, C), BF), pltpu.VMEM((FF, C), BF), pltpu.SemaphoreType.DMA]
    return call(kernel, me, [r, mask, small], outs, held=bufs, scratch=scratch, flops=24 * rows * C * C)


def pack_outs(shards, count, relative):
    if relative:
        return [shape((4, count, C), BF)] * 2
    return [shape((shards, count, C), BF)]


def send_pack(dw, outs, rows, sem):
    each = len(outs) == 2
    copies = []
    for i, out in enumerate(outs):
        src = dw.at[pl.ds(4 * i, 4), rows] if each else dw.at[:, rows]
        copies.append(pltpu.make_async_copy(src, out.at[:, rows], sem))
    for copy in copies:
        copy.start()
    return copies


def ffn_backward(sizes, me, relative, dy, r, n2, g, slope, o, mask, small, w_ffn, w_att, first, deps):
    globals_, locals_, shards = sizes
    windows = 4 * globals_ + locals_
    rows = windows * CELL
    part = C // shards
    deep = FF // shards
    count = 4 * part + deep + part
    chunks = chunks_of(rows)
    packs = pack_outs(shards, count, relative)
    n_ffn, n_att = len(w_ffn), len(w_att)

    def kernel(me_ref, feeds, sends, held, dw_out, w1, w2, wp, dw, dyl, dh, acc, acc1, sem, sem2):
        dy_in, r_in, n_in, g_in, s_in, o_in, m_in, small_in = feeds
        dr_out, do_out, ds_out = sends
        dr_ref, do_ref, ds_ref = [v.ref for v in sends]
        dy_in.start()
        m_in.start()
        copies = start_weights(held[:n_ffn], me_ref, ffn_plan(part, deep, w1, w2), sem)
        for i, here in enumerate(chunks):
            s_in.start(i, here)
        copies += start_weights(
            held[n_ffn : n_ffn + n_att], me_ref, [(first + 3 * part, part, rows_of(wp, 0, part))], sem
        )
        small_in.start()
        acc[...] = jnp.zeros_like(acc)
        acc1[...] = jnp.zeros_like(acc1)
        dy_ref = dy_in.wait()
        mask_ref = m_in.wait()

        def step(i):
            here = pl.ds(i * CELL, CELL)
            d = dy_ref[here, :] * wide(mask_ref[here, :])
            dyl[here, :] = d.astype(BF)
            acc[2] += fold8(d)

        several(windows, NORM_UNROLL, step)
        for feed in (n_in, g_in, r_in, o_in):
            feed.start()
        for copy in copies:
            copy.wait()
        for i, here in enumerate(chunks):
            s_ref = s_in.wait(i)
            for t in range(FF // C):
                cols = slice(t * C, (t + 1) * C)
                d = mm_nt(dyl[here, :], w2[cols, :]) * s_ref[here, cols].astype(F32)
                acc1[:, cols] += fold8(d)
                dh[here, cols] = d.astype(BF)
            dn = None
            for t in range(FF // C):
                one = mm_nt(dh[here, t * C : (t + 1) * C], w1[t])
                dn = one if dn is None else dn + one
            dr_ref[here, :] = dn

        n_ref = n_in.wait()
        g_ref = g_in.wait()
        for t in range(FF // C):
            cols = slice(t * C, (t + 1) * C)
            one = mm_tn(n_ref[...], dh[:, cols]).astype(BF)
            for d in range(shards):
                dw[slot_of(d, me_ref, relative), t * part : (t + 1) * part, :] = one[d * part : (d + 1) * part]
            two = mm_tn(g_ref[:, cols], dyl[...]).astype(BF)
            for d in range(C // deep):
                here = pl.ds(4 * part, deep)
                dw[slot_of(t * (C // deep) + d, me_ref, relative), here, :] = two[d * deep : (d + 1) * deep]
        going = send_pack(dw, dw_out, pl.ds(0, 4 * part + deep), sem2)

        small_ref = small_in.wait()
        gain = small_ref[G_ROW + 1 : G_ROW + 2]
        r_ref = r_in.wait()

        def step(i):
            here = pl.ds(i * CELL, CELL)
            dn = dr_ref[here, :]
            xhat, rstd = norm_parts(r_ref[here, :])
            acc[0] += fold8(dn * xhat)
            acc[1] += fold8(dn)
            dr = norm_back(dn, xhat, rstd, gain) + dy_ref[here, :] * wide(mask_ref[here, :])
            acc[3] += fold8(dr)
            dr_ref[here, :] = dr
            dyl[here, :] = dr.astype(BF)

        several(windows, NORM_UNROLL, step)
        dr_out.start()
        for i, here in enumerate(chunks):
            do_ref[here, :] = mm_nt(dyl[here, :], wp[0]).astype(BF)
            do_out.start(i, here)
        o_ref = o_in.wait()
        one = mm_tn(o_ref[...], dyl[...]).astype(BF)
        for d in range(shards):
            dw[slot_of(d, me_ref, relative), 4 * part + deep :, :] = one[d * part : (d + 1) * part]
        going += send_pack(dw, dw_out, pl.ds(4 * part + deep, part), sem2)
        for i in range(3):
            ds_ref[i : i + 1, :] = jnp.sum(acc[i], axis=0, keepdims=True)
        for t in range(FF // C):
            ds_ref[3 + t : 4 + t, :] = jnp.sum(acc1[:, t * C : (t + 1) * C], axis=0, keepdims=True)
        ds_ref[7:8, :] = jnp.sum(acc[3], axis=0, keepdims=True)
        ds_out.start()
        for copy in going:
            copy.wait()

    outs = [shape((rows, C), F32), shape((rows, C), BF), shape((8, C), F32)]
    scratch = [
        pltpu.VMEM((FF // C, C, C), BF),
        pltpu.VMEM((FF, C), BF),
        pltpu.VMEM((1, C, C), BF),
        pltpu.VMEM((shards, count, C), BF),
        pltpu.VMEM((rows, C), BF),
        pltpu.VMEM((rows, FF), BF),
        pltpu.VMEM((4, 8, C), F32),
        pltpu.VMEM((8, FF), F32),
        pltpu.SemaphoreType.DMA,
        pltpu.SemaphoreType.DMA,
    ]
    return call(
        kernel, me, [dy, r, n2, g, slope, o, mask, small], outs, held=[*w_ffn, *w_att, *deps], packs=packs,
        scratch=scratch, flops=40 * rows * C * C,
    )


def mix_backward(sizes, kind, q, k, v, p, do, mask, me, deps):
    globals_, locals_, _ = sizes
    windows = 4 * globals_ + locals_
    rows = windows * CELL

    def kernel(me_ref, feeds, sends, held, packs, acc, slope):
        q_in, k_in, v_in, p_in, do_in, m_in = feeds
        q_ref, k_ref, v_ref, p_ref, do_ref, mask_ref = [v.ref for v in feeds]
        dq, dk, dv, ds_ref = [v.ref for v in sends]
        order = (v_in, do_in, p_in, q_in, k_in, m_in) if kind == 0 else (q_in, do_in, p_in, v_in, k_in, m_in)
        for feed in order:
            feed.start()
        acc[...] = jnp.zeros_like(acc)
        if kind == 0:
            spatial_backward(
                q_ref, k_ref, v_ref, p_ref, do_ref, dq, dk, dv, acc, slope, windows,
                [feed.wait for feed in order], [send.start for send in sends[:3]],
            )
        else:
            channel_backward(
                q_ref, k_ref, v_ref, mask_ref, p_ref, do_ref, dq, dk, dv, acc, slope, globals_, locals_,
                [feed.wait for feed in order], [send.start for send in sends[:3]],
            )
        for t in range(2):
            ds_ref[t : t + 1, :] = jnp.sum(acc[t], axis=0, keepdims=True)
        ds_ref[2:8, :] = jnp.zeros((6, C), F32)
        sends[3].start()

    low = shape((rows, C), BF)
    return call(
        kernel, me, [q, k, v, p, do, mask], [low, low, low, shape((8, C), F32)], held=deps,
        scratch=[pltpu.VMEM((2, 8, C), F32), pltpu.VMEM(p.shape, BF)], flops=16 * rows * C * C,
    )


def attention_backward(sizes, me, relative, dr, u, c, n1, dq, dk, dv, ds_ffn, ds_mix, mask, small, bufs, first, deps):
    globals_, locals_, shards = sizes
    windows = 4 * globals_ + locals_
    rows = windows * CELL
    part = C // shards
    count = 3 * part + TAB
    chunks = chunks_of(rows)
    packs = pack_outs(shards, count, relative)

    def kernel(me_ref, feeds, sends, held, dw_out, w, dw, dn, acc, acck, tab, sem, sem2):
        dr_in, u_in, c_in, n_in, dq_in, dk_in, dv_in, ffn_in, mix_in, m_in, small_in = feeds
        dr_ref, u_ref, c_ref, n_ref, dq, dk, dv, ffn_ref, mix_ref, mask_ref, small_ref = [v.ref for v in feeds]
        du_ref = sends[0].ref
        plan = [(first + i * part, part, rows_of(w, i, part)) for i in range(3)]
        copies = start_weights(held[: len(bufs)], me_ref, plan, sem)
        for i, here in enumerate(chunks):
            for feed in (dq_in, dk_in, dv_in):
                feed.start(i, here)
        for feed in (c_in, dr_in, m_in, small_in, u_in, n_in, ffn_in, mix_in):
            feed.start()
        acc[...] = jnp.zeros_like(acc)
        for copy in copies:
            copy.wait()
        for i, here in enumerate(chunks):
            for feed in (dq_in, dk_in, dv_in):
                feed.wait(i)
            total = mm_nt(dq[here, :], w[0]) + mm_nt(dk[here, :], w[1]) + mm_nt(dv[here, :], w[2])
            dn[tiles_of(here)] = total.reshape(here.size // 8, 8, C)

        for feed in (c_in, dr_in, m_in, small_in):
            feed.wait()
        gain = small_ref[G_ROW : G_ROW + 1]

        def step(i):
            here = pl.ds(i * CELL, CELL)
            tiles = pl.ds(i * 8, 8)
            d = dn[tiles].reshape(CELL, C)
            xhat, rstd = norm_parts(c_ref[tiles].reshape(CELL, C))
            acc[0] += fold8(d * xhat)
            acc[1] += fold8(d)
            dc = norm_back(d, xhat, rstd, gain) + dr_ref[here, :]
            dn[tiles] = (dc * wide(mask_ref[here, :])).reshape(8, 8, C)

        several(windows, NORM_UNROLL, step)
        u_in.wait()
        conv_backward(dn, u_ref, du_ref, small_ref, acck, globals_, locals_)
        sends[0].start()

        ffn_in.wait()
        mix_in.wait()
        rows_ = [jnp.sum(acck[t], axis=0, keepdims=True) for t in range(10)]
        rows_ += [jnp.sum(acc[1], axis=0, keepdims=True), mix_ref[0:1, :], mix_ref[1:2, :], ffn_ref[7:8, :]]
        rows_ += [ffn_ref[1:2, :], ffn_ref[2:3, :], jnp.sum(acc[0], axis=0, keepdims=True), ffn_ref[0:1, :]]
        rows_ += [ffn_ref[3 + t : 4 + t, :] for t in range(FF // C)]
        tab[...] = jnp.zeros_like(tab)
        for t, row in enumerate(rows_):
            tab[t : t + 1, :] = row
        low = tab[...].astype(BF)
        for d in range(shards):
            dw[d, 3 * part :, :] = low
        going = send_pack(dw, dw_out, pl.ds(3 * part, TAB), sem2)

        n_in.wait()
        for i, right in enumerate((dq, dk, dv)):
            one = mm_tn(n_ref[...], right[...]).astype(BF)
            for d in range(shards):
                dw[slot_of(d, me_ref, relative), i * part : (i + 1) * part, :] = one[d * part : (d + 1) * part]
            going += send_pack(dw, dw_out, pl.ds(i * part, part), sem2)
        for copy in going:
            copy.wait()

    outs = [shape((windows * 8, 8, C), F32)]
    scratch = [
        pltpu.VMEM((3, C, C), BF),
        pltpu.VMEM((shards, count, C), BF),
        pltpu.VMEM((windows * 8, 8, C), F32),
        pltpu.VMEM((2, 8, C), F32),
        pltpu.VMEM((10, 8, C), F32),
        pltpu.VMEM((TAB, C), F32),
        pltpu.SemaphoreType.DMA,
        pltpu.SemaphoreType.DMA,
    ]
    return call(
        kernel, me, [dr, u, c, n1, dq, dk, dv, ds_ffn, ds_mix, mask, small], outs, held=[*bufs, *deps],
        packs=packs, scratch=scratch, flops=20 * rows * C * C,
    )


def join(values, deps):
    values, deps = list(values), list(deps)

    def kernel(*refs):
        pass

    return pl.pallas_call(
        kernel,
        out_shape=[shape(v.shape, v.dtype) for v in values],
        in_specs=[HELD] * (len(values) + len(deps)),
        out_specs=[HELD] * len(values),
        input_output_aliases={i: i for i in range(len(values))},
    )(*values, *deps)


def to_cells(glob, loc):
    count = glob.shape[0]
    wins = glob.reshape(count, 2, WIN, 2, WIN, C).transpose(0, 1, 3, 2, 4, 5).reshape(count * 4, WIN, WIN, C)
    both = jnp.concatenate([wins, loc], axis=0)
    return jnp.pad(both, ((0, 0), (0, 1), (0, 1), (0, 0))).astype(F32)


def from_cells(cells, globals_):
    cells = cells.reshape(-1, 8, 8, C)[:, :WIN, :WIN]
    wins = cells[: globals_ * 4].reshape(globals_, 2, 2, WIN, WIN, C)
    return wins.transpose(0, 1, 3, 2, 4, 5).reshape(globals_, SIDE, SIDE, C), cells[globals_ * 4 :]


def cell_mask(extent, globals_):
    places = jnp.arange(8, dtype=jnp.int32)
    size = jnp.concatenate([jnp.full((globals_ * 4, 2), WIN, jnp.int32), extent.astype(jnp.int32)], axis=0)
    rows = places[None, :, None] < size[:, 0][:, None, None]
    cols = places[None, None, :] < size[:, 1][:, None, None]
    return jnp.logical_and(rows, cols).astype(F32)


def layer(sizes, me, tokens, cotangent, mask4, w_att, w_ffn, offsets, relative, plan):
    windows = 4 * sizes[0] + sizes[1]
    rows = windows * CELL
    mask = jnp.broadcast_to(mask4.reshape(rows, 1), (rows, LANES))
    u = (tokens * mask4[..., None]).reshape(windows * 8, 8, C)
    dy = cotangent.reshape(rows, C)
    kept = []
    for b in range(2):
        r, small, *att = attention_forward(sizes, b, me, u, mask, w_att[b], offsets[b])
        w_ffn[b] = plan.late_weights(b, w_ffn[b], r)
        x, *ffn = ffn_forward(sizes, me, r, mask, small, w_ffn[b])
        kept.append((u, r, small, att, ffn))
        u = x.reshape(windows * 8, 8, C)
    out = u
    for b in (1, 0):
        u, r, small, (c, n1, q, k, v, o, p), ffn = kept[b]
        dr, do, ds_ffn, *dw = ffn_backward(
            sizes, me, relative[b], dy, r, *ffn, o, mask, small, w_ffn[b], w_att[b], offsets[b], plan.deps(b, 0)
        )
        plan.ffn_pack(b, dw)
        dq, dk, dv, ds_mix = mix_backward(sizes, b, q, k, v, p, do, mask, me, plan.deps(b, 1))
        du, *dw = attention_backward(
            sizes, me, relative[b], dr, u, c, n1, dq, dk, dv, ds_ffn, ds_mix, mask, small, w_att[b], offsets[b],
            plan.deps(b, 2),
        )
        plan.att_pack(b, dw)
        dy = du.reshape(rows, C)
    return out, du * mask4.reshape(windows * 8, 8, 1)


def xor(v, axis, turn):
    size = lax.axis_size(axis)
    return lax.ppermute(v, axis, [(i, i ^ turn) for i in range(size)])


def gather_near(own):
    return [own, xor(own, "fsdp", 2), xor(own, "fsdp", 4), xor(own, "fsdp", 6)]


def gather_core(near):
    out = []
    for v in near:
        out += [v, xor(v, "fsdp", 1)]
    return out


def add(*terms):
    total = terms[0].astype(F32)
    for term in terms[1:]:
        total = total + term.astype(F32)
    return total.astype(BF)


class Direct:
    def __init__(self):
        self.sums = {}

    def late_weights(self, b, bufs, r):
        return gather_core(join(bufs, [r])) if b == 0 else bufs

    def core(self, pack):
        keep, send = pack
        got = xor(send, "fsdp", 1)
        return [add(keep[i], got[i]) for i in range(4)]

    def chips(self, parts):
        own, *away = parts
        return add(own, *[xor(v, "fsdp", 2 * i + 2) for i, v in enumerate(away)])

    def ffn_pack(self, b, dw):
        self.sums[b, "f"] = self.core(dw)

    def att_pack(self, b, dw):
        self.sums[b, "a"] = self.core(dw)

    def deps(self, b, stage):
        if b == 1 and stage == 2:
            return self.sums[1, "f"]
        if b == 0 and stage == 1:
            self.own_ffn = self.chips(self.sums[1, "f"])
            return [self.own_ffn] + self.sums[1, "a"]
        if b == 0 and stage == 2:
            self.own_att = self.chips(self.sums[1, "a"])
            return [self.own_att] + self.sums[0, "f"]
        return []

    def results(self):
        far = lax.psum((self.own_ffn, self.own_att), "dp")
        near = [self.chips(self.sums[0, "f"]), self.chips(self.sums[0, "a"])]
        for turn in (1, 2):
            near = [add(v, xor(v, "dp", turn)) for v in near]
        return [near, far]


class Plain:
    def __init__(self):
        self.packs = [[None, None], [None, None]]

    def late_weights(self, b, bufs, r):
        return bufs

    def ffn_pack(self, b, dw):
        self.packs[b][0] = dw[0]

    def att_pack(self, b, dw):
        self.packs[b][1] = dw[0]

    def deps(self, b, stage):
        return []

    def results(self):
        return [
            lax.psum([lax.psum_scatter(v, "fsdp", scatter_dimension=0, tiled=True)[0] for v in pair], "dp")
            for pair in self.packs
        ]


def body(
    global_tokens,
    local_tokens,
    crop_extent,
    conv_weight,
    vectors,
    gains,
    qkv_weight,
    proj_weight,
    fc1_weight,
    fc1_bias,
    fc2_weight,
    global_cotangent,
    local_cotangent,
):
    shards = lax.axis_size("fsdp")
    direct = shards == 8 and lax.axis_size("dp") == 4
    part = C // shards
    globals_, locals_ = global_tokens.shape[0], local_tokens.shape[0]
    sizes = (globals_, locals_, shards)
    index = lax.axis_index("fsdp")
    me = index.astype(jnp.int32).reshape(1)

    own_small = jnp.concatenate([conv_weight, vectors, gains], axis=1)
    own_bias = fc1_bias.reshape(2, 1, FF // shards)
    w_att, w_ffn = [], []
    for b in range(2):
        cols = lambda w, n: [w[b][:, i * C : (i + 1) * C] for i in range(n)]
        table = jnp.zeros((TAB, C), BF)
        table = lax.dynamic_update_slice(table, own_small[b], (0, index * part))
        start = index * (FF // shards)
        table = lax.dynamic_update_slice(table, own_bias[b], (B_ROW + start // C, start % C))
        att = cols(qkv_weight, 3) + [proj_weight[b], table]
        ffn = cols(fc1_weight, 4) + [fc2_weight[b]]
        if b == 0 and direct:
            w_att.append(gather_core(gather_near(jnp.concatenate(att, axis=0))))
            w_ffn.append(gather_near(jnp.concatenate(ffn, axis=0)))
        else:
            whole = lax.all_gather(jnp.concatenate(ffn + att, axis=0), "fsdp", axis=0)
            w_ffn.append([whole])
            w_att.append([whole])
    offsets = [0 if direct else 4 * part + FF // shards, 4 * part + FF // shards]

    plan = Direct() if direct else Plain()
    mask4 = cell_mask(crop_extent, globals_)
    out, grad = layer(
        sizes, me,
        to_cells(global_tokens, local_tokens),
        to_cells(global_cotangent, local_cotangent),
        mask4, w_att, w_ffn, offsets, (direct, direct), plan,
    )
    out = from_cells(out.astype(BF), globals_)
    grad = from_cells(grad, globals_)
    grads = plan.results()
    deep = FF // shards

    def cut(half, start, n):
        return jnp.stack(
            [
                jnp.concatenate([g[half][(start + i) * part : (start + i + 1) * part] for i in range(n)], axis=1)
                for g in grads
            ]
        ).astype(F32)

    table = jnp.stack([g[1][3 * part :] for g in grads]).astype(F32)
    main = lax.dynamic_slice(table, (0, 0, index * part), (2, 18, part))
    bias = lax.dynamic_slice(table[:, 18:22].reshape(2, FF), (0, index * deep), (2, deep))
    fc2 = jnp.stack([g[0][4 * part : 4 * part + deep] for g in grads]).astype(F32)
    proj = jnp.stack([g[0][4 * part + deep :] for g in grads]).astype(F32)
    return (
        out[0], out[1], grad[0], grad[1],
        main[:, 0:9], main[:, 9:16], main[:, 16:18],
        cut(1, 0, 3), proj, cut(0, 0, 4), bias, fc2,
    )


def solution(mesh):
    crops = P(("dp", "fsdp"), None, None, None)
    last = P(None, None, "fsdp")
    middle = P(None, "fsdp", None)
    return jax.shard_map(
        body,
        mesh=mesh,
        in_specs=(
            crops, crops, P(("dp", "fsdp"), None), last, last, last, middle, middle, middle,
            P(None, "fsdp"), middle, crops, crops,
        ),
        out_specs=(
            crops, crops, crops, crops, last, last, last, middle, middle, middle, P(None, "fsdp"), middle,
        ),
        check_vma=False,
    )
```

time: 599 us -> 424 us (0.71)
  waiting for transfers between devices: 238 us -> 152 us
  Pallas kernels: 242 us -> 166 us
  blocking collectives: 40 us -> 0 us
  starting transfers between devices: 0.46 us -> 35.7 us
  local copies, waits for them, and re-layouts: 35.7 us -> 18 us
    ppermute x0 -> x34, waiting for transfers between devices: none -> 114 us  [xor(): return lax.ppermute(v, axis, [(i, i ^ turn) for i in range(size)])]
    pallas_call x8 -> x11, Pallas kernels: 242 us -> 166 us  [the longest x10 166 us: call(): pl.pallas_call(body, out_shape=list(outs) + list(packs), in_specs=[pl.Blo...]
    unnamed x9 -> x2, waiting for transfers between devices: 68.3 us -> 0.42 us
    all_gather x2 -> x1, waiting for transfers between devices: 61.9 us -> 0.02 us  [body(): whole = lax.all_gather(jnp.concatenate(ffn + att, axis=0), 'fsdp', axis=0)]
    reduce_scatter x2 -> x0, waiting for transfers between devices: 58.3 us -> none  [body(): own = lax.psum_scatter(both, 'fsdp', scatter_dimension=0, tiled=True)[0]]
    ppermute x0 -> x34, starting transfers between devices: none -> 35.3 us  [xor(): return lax.ppermute(v, axis, [(i, i ^ turn) for i in range(size)])]
    all_gather x2 -> x0, blocking collectives: 20.6 us -> none  [the longest x1 10.3 us: body(): lax.all_gather(fc1_bias, 'fsdp', axis=1, tiled=True).reshape(2, FF // C, C)]
    convert_element_type x3 -> x17, other arithmetic: 2.13 us -> 21.7 us  [the longest x12 17.9 us: add(): return total.astype(BF)]
  transfers between devices with their start and end apart: 7 -> 36, of which waited for: 6 -> 19; matrix products, arithmetic and copies ran while one was open for 5% -> 7% of each run, Pallas kernels for 13% -> 12%
where the time goes in v2:
time: 424 us; the launch traced here: 416 us
  Pallas kernels  166 us (39%)
  waiting for transfers between devices  152 us (36%)
  starting transfers between devices  35.7 us (8%)
  other arithmetic  28.7 us (7%)
  local copies, waits for them, and re-layouts  18 us (4%)
  between operations  15.5 us (4%)
    pallas_call x10, Pallas kernels, call(): pl.pallas_call(body, out_shape=list(outs) + list(packs), in_specs=[pl.Blo...  166 us
    ppermute x34, waiting for transfers between devices, xor(): return lax.ppermute(v, axis, [(i, i ^ turn) for i in range(size)])  114 us
    psum x1, waiting for transfers between devices, results(): far = lax.psum((self.own_ffn, self.own_att), 'dp')  38 us
    ppermute x34, starting transfers between devices, xor(): return lax.ppermute(v, axis, [(i, i ^ turn) for i in range(size)])  35.3 us
    convert_element_type x12, other arithmetic, add(): return total.astype(BF)  17.9 us
  transfers between devices with their start and end apart: 36, of which 19 were waited for; matrix products, arithmetic and copies ran while one was open for 7% of the time, Pallas kernels for 12%

profile of v2, /device:TPU:0, one launch (start us, length us, event | category | flops | bytes accessed | tf_op | source)
XLA Modules:
  0.0 415.9 jit_solution(18119596906927627192)
XLA Ops:
  23.3 6.3 %collective-permute-done.3.refs_6_.refs_20_.refs_15_ = bf16[288,512]{1,0:T(8,128)(2,1)} collective-permute-done((bf16[288,512]{1,0:T(8,128)(2,1)S(1)}, bf16[288,512]{1,0:T(8,128)(2,1)}, u32[]{:S(2)}, u32[]{:S(2)}) %collective-permute-start.3) | collective-permute-done | bytes 294944 | tf_op jit(solution)/shard_map/ppermute | solution.py:914
  29.6 7.2 %collective-permute-done.5.refs_8_.refs_22_.refs_17_ = bf16[288,512]{1,0:T(8,128)(2,1)} collective-permute-done((bf16[288,512]{1,0:T(8,128)(2,1)S(1)}, bf16[288,512]{1,0:T(8,128)(2,1)}, u32[]{:S(2)}, u32[]{:S(2)}) %collective-permute-start.5) | collective-permute-done | bytes 294944 | tf_op jit(solution)/shard_map/ppermute | solution.py:914
  44.2 16.5 %shard_map.220 = (f32[1344,512]{1,0:T(8,128)}, f32[32,512]{1,0:T(8,128)}, f32[168,8,512]{2,1,0:T(8,128)}, bf16[1344,512]{1,0:T(8,128)(2,1)}, bf16[1344,512]{1,0:...) custom-call(s32[1]{0:T(128)} %bitcast.me_ref, ...), custom_call_target="tpu_custom_call" | custom-call | flops 4227858432 | bytes 20971520 | tf_op jit(solution)/shard_map/pallas_call | solution.py:84
  60.7 5.0 %collective-permute-done.8.refs_2_ = bf16[512,512]{1,0:T(8,128)(2,1)} collective-permute-done((bf16[512,512]{1,0:T(8,128)(2,1)S(1)}, bf16[512,512]{1,0:T(8,128)(2,1)}, u32[]{:S(2)}, u32[]{:S(2)}) %collective-permute-start.8) | collective-permute-done | bytes 524320 | tf_op jit(solution)/shard_map/ppermute | solution.py:914
  65.7 7.4 %collective-permute-done.9.refs_3_ = bf16[512,512]{1,0:T(8,128)(2,1)} collective-permute-done((bf16[512,512]{1,0:T(8,128)(2,1)S(1)}, bf16[512,512]{1,0:T(8,128)(2,1)}, u32[]{:S(2)}, u32[]{:S(2)}) %collective-permute-start.9) | collective-permute-done | bytes 524320 | tf_op jit(solution)/shard_map/ppermute | solution.py:914
  78.3 15.9 %shard_map.222 = (f32[1344,512]{1,0:T(8,128)}, bf16[1344,512]{1,0:T(8,128)(2,1)}, bf16[1344,2048]{1,0:T(8,128)(2,1)}, bf16[1344,2048]{1,0:T(8,128)(2,1)}) custom-call(s32[1]{0:T(128)} %bitcast.me_ref, f32[1344,512]{1,0:T(8,128)} %get-tuple-element.66.refs_4_.refs_0_.refs_1_, f32[1344,128]{1,0:T(8,128)} %broadcast_in_dim.2.refs_1_.refs_6_.refs_5_.refs_9_, ...), custom_call_target="tpu_custom_call" | custom-call | flops 8455716864 | bytes 20971520 | tf_op jit(solution)/shard_map/pallas_call | solution.py:84
  94.2 13.0 %shard_map.223 = (f32[1344,512]{1,0:T(8,128)}, f32[32,512]{1,0:T(8,128)}, f32[168,8,512]{2,1,0:T(8,128)}, bf16[1344,512]{1,0:T(8,128)(2,1)}, bf16[1344,512]{1,0:...) custom-call(s32[1]{0:T(128)} %bitcast.me_ref, ...), custom_call_target="tpu_custom_call" | custom-call | flops 4227858432 | bytes 20971520 | tf_op jit(solution)/shard_map/pallas_call | solution.py:84
  107.2 15.6 %shard_map.224 = (f32[1344,512]{1,0:T(8,128)}, bf16[1344,512]{1,0:T(8,128)(2,1)}, bf16[1344,2048]{1,0:T(8,128)(2,1)}, bf16[1344,2048]{1,0:T(8,128)(2,1)}) custom-call(s32[1]{0:T(128)} %bitcast.me_ref, f32[1344,512]{1,0:T(8,128)} %get-tuple-element.73.refs_0_.refs_1_, f32[1344,128]{1,0:T(8,128)} %broadcast_in_dim.2.refs_1_.refs_6_.refs_5_.refs_9_, ...), custom_call_target="tpu_custom_call" | custom-call | flops 8455716864 | bytes 20971520 | tf_op jit(solution)/shard_map/pallas_call | solution.py:84
  122.8 24.3 %shard_map.225 = (f32[1344,512]{1,0:T(8,128)}, bf16[1344,512]{1,0:T(8,128)(2,1)}, f32[8,512]{1,0:T(8,128)}, bf16[4,576,512]{2,1,0:T(8,128)(2,1)}, bf16[4,576,512]{2,1,0:T(8,128)(2,1)}) custom-call(s32[1]{0:T(128)} %bitcast.me_ref, f32[1344,512]{1,0:T(8,128)} %bitcast_convert_fusion.refs_0_, f32[1344,512]{1,0:T(8,128)} %get-tuple-element.73.refs_0_.refs_1_, ...), custom_call_target="tpu_custom_call" | custom-call | flops 14092861440 | bytes 20971520 | tf_op jit(solution)/shard_map/pallas_call | solution.py:84
  158.4 8.0 %shard_map.226 = (bf16[1344,512]{1,0:T(8,128)(2,1)}, bf16[1344,512]{1,0:T(8,128)(2,1)}, bf16[1344,512]{1,0:T(8,128)(2,1)}, f32[8,512]{1,0:T(8,128)}) custom-call(s32[1]{0:T(128)} %bitcast.me_ref, bf16[1344,512]{1,0:T(8,128)(2,1)} %get-tuple-element.83.refs_0_, bf16[1344,512]{1,0:T(8,128)(2,1)} %get-tuple-element.84.refs_1_, ...), custom_call_target="tpu_custom_call" | custom-call | flops 5637144576 | bytes 20971520 | tf_op jit(solution)/shard_map/pallas_call | solution.py:84
  166.4 5.7 %collective-permute-done.17 = bf16[576,512]{1,0:T(8,128)(2,1)} collective-permute-done((bf16[576,512]{1,0:T(8,128)(2,1)S(1)}, bf16[576,512]{1,0:T(8,128)(2,1)}, u32[]{:S(2)}, u32[]{:S(2)}) %collective-permute-start.17) | collective-permute-done | bytes 589856 | tf_op jit(solution)/shard_map/ppermute | solution.py:914
  172.1 11.8 %collective-permute-done.16 = bf16[576,512]{1,0:T(8,128)(2,1)} collective-permute-done((bf16[576,512]{1,0:T(8,128)(2,1)S(1)}, bf16[576,512]{1,0:T(8,128)(2,1)}, u32[]{:S(2)}, u32[]{:S(2)}) %collective-permute-start.16) | collective-permute-done | bytes 589856 | tf_op jit(solution)/shard_map/ppermute | solution.py:914
  187.1 18.1 %shard_map.227 = (f32[168,8,512]{2,1,0:T(8,128)}, bf16[4,224,512]{2,1,0:T(8,128)(2,1)}, bf16[4,224,512]{2,1,0:T(8,128)(2,1)}) custom-call(s32[1]{0:T(128)} %bitcast.me_ref, f32[1344,512]{1,0:T(8,128)} %get-tuple-element.80.refs_0_, f32[168,8,512]{2,1,0:T(8,128)} %bitcast.132, f32[168,8,512]{2,1,0:T(8,128)} %get-tuple-element.81.refs_2_, ...), custom_call_target="tpu_custom_call" | custom-call | flops 7046430720 | bytes 20971520 | tf_op jit(solution)/shard_map/pallas_call | solution.py:84
  205.2 24.5 %shard_map.228 = (f32[1344,512]{1,0:T(8,128)}, bf16[1344,512]{1,0:T(8,128)(2,1)}, f32[8,512]{1,0:T(8,128)}, bf16[4,576,512]{2,1,0:T(8,128)(2,1)}, bf16[4,576,512]{2,1,0:T(8,128)(2,1)}) custom-call(s32[1]{0:T(128)} %bitcast.me_ref, f32[1344,512]{1,0:T(8,128)} %bitcast.133, f32[1344,512]{1,0:T(8,128)} %get-tuple-element.66.refs_4_.refs_0_.refs_1_, ...), custom_call_target="tpu_custom_call" | custom-call | flops 14092861440 | bytes 20971520 | tf_op jit(solution)/shard_map/pallas_call | solution.py:84
  230.4 5.2 %collective-permute-done.18 = bf16[4,224,512]{2,1,0:T(8,128)(2,1)} collective-permute-done((bf16[4,224,512]{2,1,0:T(8,128)(2,1)}, bf16[4,224,512]{2,1,0:T(8,128)(2,1)}, u32[]{:S(2)}, u32[]{:S(2)}) %collective-permute-start.18) | collective-permute-done | bytes 917536 | tf_op jit(solution)/shard_map/ppermute | solution.py:914
  253.2 11.6 %shard_map.229 = (bf16[1344,512]{1,0:T(8,128)(2,1)}, bf16[1344,512]{1,0:T(8,128)(2,1)}, bf16[1344,512]{1,0:T(8,128)(2,1)}, f32[8,512]{1,0:T(8,128)}) custom-call(s32[1]{0:T(128)} %bitcast.me_ref, bf16[1344,512]{1,0:T(8,128)(2,1)} %get-tuple-element.103.refs_0_, bf16[1344,512]{1,0:T(8,128)(2,1)} %get-tuple-element.104.refs_1_, ...), custom_call_target="tpu_custom_call" | custom-call | flops 5637144576 | bytes 20971520 | tf_op jit(solution)/shard_map/pallas_call | solution.py:84
  264.8 11.3 %collective-permute-done.30 = bf16[576,512]{1,0:T(8,128)(2,1)} collective-permute-done((bf16[576,512]{1,0:T(8,128)(2,1)}, bf16[576,512]{1,0:T(8,128)(2,1)}, u32[]{:S(2)}, u32[]{:S(2)}) %collective-permute-start.30) | collective-permute-done | bytes 589856 | tf_op jit(solution)/shard_map/ppermute | solution.py:914
  279.1 18.1 %shard_map.230 = (f32[168,8,512]{2,1,0:T(8,128)}, bf16[4,224,512]{2,1,0:T(8,128)(2,1)}, bf16[4,224,512]{2,1,0:T(8,128)(2,1)}) custom-call(s32[1]{0:T(128)} %bitcast.me_ref, f32[1344,512]{1,0:T(8,128)} %get-tuple-element.100.refs_0_, f32[168,8,512]{2,1,0:T(8,128)} %bitcast.119, f32[168,8,512]{2,1,0:T(8,128)} %get-tuple-element.101.refs_2_, ...), custom_call_target="tpu_custom_call" | custom-call | flops 7046430720 | bytes 20971520 | tf_op jit(solution)/shard_map/pallas_call | solution.py:84
  307.5 14.0 %collective-permute-done.32 = bf16[576,512]{1,0:T(8,128)(2,1)} collective-permute-done((bf16[576,512]{1,0:T(8,128)(2,1)}, bf16[576,512]{1,0:T(8,128)(2,1)}, u32[]{:S(2)}, u32[]{:S(2)}) %collective-permute-start.32) | collective-permute-done | bytes 589856 | tf_op jit(solution)/shard_map/ppermute | solution.py:914
  322.9 6.3 %collective-permute-start.33 = (bf16[576,512]{1,0:T(8,128)(2,1)S(1)}, bf16[576,512]{1,0:T(8,128)(2,1)S(1)}, u32[]{:S(2)}, u32[]{:S(2)}) collective-permute-start(bf16[576,512]{1,0:T(8,128)(2,1)S(1)} %add_convert_fusion.1), channel_id=1, source_target_pairs={{0,16},{8,24},{16,0},{24,8},{1,17},{9,25},{17,1},{25,9},{2,18},{10... | collective-permute-start | bytes 1769480 | tf_op jit(solution)/shard_map/ppermute | solution.py:914
  329.2 38.0 %all-reduce.6.cloned.1.call-done = (bf16[224,512]{1,0:T(8,128)(2,1)}, bf16[576,512]{1,0:T(8,128)(2,1)}) async-done(((bf16[224,512]{1,0:T(8,128)(2,1)}, bf16[576,512]{1,0:T(8,128)(2,1)}), (bf16[224,512]{1,0:T(8,128)(2,1)}, bf16[576,512]{1,0:T(8,128)(2,1)})) %all-reduce.6.cloned.1.call-update) | async-done | bytes 819216 | tf_op jit(solution)/shard_map/psum | solution.py:969
  374.7 5.9 %collective-permute-done.26 = bf16[224,512]{1,0:T(8,128)(2,1)S(1)} collective-permute-done((bf16[224,512]{1,0:T(8,128)(2,1)S(1)}, bf16[224,512]{1,0:T(8,128)(2,1)S(1)}, u32[]{:S(2)}, u32[]{:S(2)}) %collective-permute-start.26) | collective-permute-done | bytes 229408 | tf_op jit(solution)/shard_map/ppermute | solution.py:914
  386.8 5.5 %collective-permute-done.27 = bf16[224,512]{1,0:T(8,128)(2,1)S(1)} collective-permute-done((bf16[224,512]{1,0:T(8,128)(2,1)S(1)}, bf16[224,512]{1,0:T(8,128)(2,1)S(1)}, u32[]{:S(2)}, u32[]{:S(2)}) %collective-permute-start.27) | collective-permute-done | bytes 229408 | tf_op jit(solution)/shard_map/ppermute | solution.py:914
  393.9 11.0 %collective-permute-done.28 = bf16[224,512]{1,0:T(8,128)(2,1)S(1)} collective-permute-done((bf16[224,512]{1,0:T(8,128)(2,1)S(1)}, bf16[224,512]{1,0:T(8,128)(2,1)S(1)}, u32[]{:S(2)}, u32[]{:S(2)}) %collective-permute-start.28) | collective-permute-done | bytes 229408 | tf_op jit(solution)/shard_map/ppermute | solution.py:914
  (209 shorter events, 94.2 us)
Async XLA Ops:
  7.2 87.0 %all-gather.3.cloned.1.call-start = ((), (), s32[]{:S(2)}) async-start(), calls=%async_computation | async-start | bytes 7372800 | tf_op jit(solution)/shard_map/all_gather | solution.py:1037
  12.0 27.1 %collective-permute-start = (bf16[288,512]{1,0:T(8,128)(2,1)S(1)}, bf16[288,512]{1,0:T(8,128)(2,1)S(1)}, u32[]{:S(2)}, u32[]{:S(2)}) collective-permute-start(bf16[288,512]{1,0:T(8,128)(2,1)S(1)} %constant_dynamic-update-slice_fusion.refs_2_.refs_16_.refs_11_), channel_id=1, source_target_pairs={{0,1},{1,0},{2,3},{3,2},{4,5},{5,4},{6,7},{7,6},{8,9},{9,8},{10,11... | collective-permute-start | bytes 884744 | tf_op jit(solution)/shard_map/ppermute | solution.py:914
  15.4 14.2 %collective-permute-start.3 = (bf16[288,512]{1,0:T(8,128)(2,1)S(1)}, bf16[288,512]{1,0:T(8,128)(2,1)}, u32[]{:S(2)}, u32[]{:S(2)}) collective-permute-start(bf16[288,512]{1,0:T(8,128)(2,1)S(1)} %constant_dynamic-update-slice_fusion.refs_2_.refs_16_.refs_11_), channel_id=1, source_target_pairs={{0,4},{1,5},{2,6},{3,7},{4,0},{5,1},{6,2},{7,3},{8,12},{9,13},{10,... | collective-permute-start | bytes 884744 | tf_op jit(solution)/shard_map/ppermute | solution.py:914
  16.7 20.1 %collective-permute-start.5 = (bf16[288,512]{1,0:T(8,128)(2,1)S(1)}, bf16[288,512]{1,0:T(8,128)(2,1)}, u32[]{:S(2)}, u32[]{:S(2)}) collective-permute-start(bf16[288,512]{1,0:T(8,128)(2,1)S(1)} %constant_dynamic-update-slice_fusion.refs_2_.refs_16_.refs_11_), channel_id=1, source_target_pairs={{0,6},{1,7},{2,4},{3,5},{4,2},{5,3},{6,0},{7,1},{8,14},{9,15},{10,... | collective-permute-start | bytes 884744 | tf_op jit(solution)/shard_map/ppermute | solution.py:914
  16.9 43.8 %collective-permute-start.7 = (bf16[512,512]{1,0:T(8,128)(2,1)S(1)}, bf16[512,512]{1,0:T(8,128)(2,1)}, u32[]{:S(2)}, u32[]{:S(2)}) collective-permute-start(bf16[512,512]{1,0:T(8,128)(2,1)S(1)} %get-tuple-element.187.refs_0_), channel_id=1, source_target_pairs={{0,2},{1,3},{2,0},{3,1},{4,6},{5,7},{6,4},{7,5},{8,10},{9,11},{10,... | collective-permute-start | bytes 1572872 | tf_op jit(solution)/shard_map/ppermute | solution.py:914
  23.3 15.9 %collective-permute-start.2 = (bf16[288,512]{1,0:T(8,128)(2,1)}, bf16[288,512]{1,0:T(8,128)(2,1)}, u32[]{:S(2)}, u32[]{:S(2)}) collective-permute-start(bf16[288,512]{1,0:T(8,128)(2,1)} %collective-permute-done.1.refs_4_.refs_18_.refs_13_), channel_id=1, source_target_pairs={{0,1},{1,0},{2,3},{3,2},{4,5},{5,4},{6,7},{7,6},{8,9},{9,8},{10,11... | collective-permute-start | bytes 884744 | tf_op jit(solution)/shard_map/ppermute | solution.py:914
  29.6 13.5 %collective-permute-start.4 = (bf16[288,512]{1,0:T(8,128)(2,1)}, bf16[288,512]{1,0:T(8,128)(2,1)}, u32[]{:S(2)}, u32[]{:S(2)}) collective-permute-start(bf16[288,512]{1,0:T(8,128)(2,1)} %collective-permute-done.3.refs_6_.refs_20_.refs_15_), channel_id=1, source_target_pairs={{0,1},{1,0},{2,3},{3,2},{4,5},{5,4},{6,7},{7,6},{8,9},{9,8},{10,11... | collective-permute-start | bytes 884744 | tf_op jit(solution)/shard_map/ppermute | solution.py:914
  39.1 26.6 %collective-permute-start.8 = (bf16[512,512]{1,0:T(8,128)(2,1)S(1)}, bf16[512,512]{1,0:T(8,128)(2,1)}, u32[]{:S(2)}, u32[]{:S(2)}) collective-permute-start(bf16[512,512]{1,0:T(8,128)(2,1)S(1)} %get-tuple-element.187.refs_0_), channel_id=1, source_target_pairs={{0,4},{1,5},{2,6},{3,7},{4,0},{5,1},{6,2},{7,3},{8,12},{9,13},{10,... | collective-permute-start | bytes 1572872 | tf_op jit(solution)/shard_map/ppermute | solution.py:914
  39.2 33.9 %collective-permute-start.9 = (bf16[512,512]{1,0:T(8,128)(2,1)S(1)}, bf16[512,512]{1,0:T(8,128)(2,1)}, u32[]{:S(2)}, u32[]{:S(2)}) collective-permute-start(bf16[512,512]{1,0:T(8,128)(2,1)S(1)} %get-tuple-element.187.refs_0_), channel_id=1, source_target_pairs={{0,6},{1,7},{2,4},{3,5},{4,2},{5,3},{6,0},{7,1},{8,14},{9,15},{10,... | collective-permute-start | bytes 1572872 | tf_op jit(solution)/shard_map/ppermute | solution.py:914
  154.8 17.3 %collective-permute-start.17 = (bf16[576,512]{1,0:T(8,128)(2,1)S(1)}, bf16[576,512]{1,0:T(8,128)(2,1)}, u32[]{:S(2)}, u32[]{:S(2)}) collective-permute-start(bf16[576,512]{1,0:T(8,128)(2,1)S(1)} %get-tuple-element.168.refs_15_), channel_id=1, source_target_pairs={{0,6},{1,7},{2,4},{3,5},{4,2},{5,3},{6,0},{7,1},{8,14},{9,15},{10,... | collective-permute-start | bytes 1769480 | tf_op jit(solution)/shard_map/ppermute | solution.py:914
  157.4 26.5 %collective-permute-start.16 = (bf16[576,512]{1,0:T(8,128)(2,1)S(1)}, bf16[576,512]{1,0:T(8,128)(2,1)}, u32[]{:S(2)}, u32[]{:S(2)}) collective-permute-start(bf16[576,512]{1,0:T(8,128)(2,1)S(1)} %get-tuple-element.169.refs_14_), channel_id=1, source_target_pairs={{0,4},{1,5},{2,6},{3,7},{4,0},{5,1},{6,2},{7,3},{8,12},{9,13},{10,... | collective-permute-start | bytes 1769480 | tf_op jit(solution)/shard_map/ppermute | solution.py:914
  158.4 25.5 %collective-permute-start.15 = (bf16[576,512]{1,0:T(8,128)(2,1)S(1)}, bf16[576,512]{1,0:T(8,128)(2,1)}, u32[]{:S(2)}, u32[]{:S(2)}) collective-permute-start(bf16[576,512]{1,0:T(8,128)(2,1)S(1)} %get-tuple-element.167.refs_13_), channel_id=1, source_target_pairs={{0,2},{1,3},{2,0},{3,1},{4,6},{5,7},{6,4},{7,5},{8,10},{9,11},{10,... | collective-permute-start | bytes 1769480 | tf_op jit(solution)/shard_map/ppermute | solution.py:914
  239.1 12.2 %collective-permute-start.20 = (bf16[224,512]{1,0:T(8,128)(2,1)S(1)}, bf16[224,512]{1,0:T(8,128)(2,1)S(1)}, u32[]{:S(2)}, u32[]{:S(2)}) collective-permute-start(bf16[224,512]{1,0:T(8,128)(2,1)S(1)} %get-tuple-element.175.refs_9_), channel_id=1, source_target_pairs={{0,4},{1,5},{2,6},{3,7},{4,0},{5,1},{6,2},{7,3},{8,12},{9,13},{10,... | collective-permute-start | bytes 688136 | tf_op jit(solution)/shard_map/ppermute | solution.py:914
  240.2 11.2 %collective-permute-start.19 = (bf16[224,512]{1,0:T(8,128)(2,1)S(1)}, bf16[224,512]{1,0:T(8,128)(2,1)S(1)}, u32[]{:S(2)}, u32[]{:S(2)}) collective-permute-start(bf16[224,512]{1,0:T(8,128)(2,1)S(1)} %get-tuple-element.173.refs_8_), channel_id=1, source_target_pairs={{0,2},{1,3},{2,0},{3,1},{4,6},{5,7},{6,4},{7,5},{8,10},{9,11},{10,... | collective-permute-start | bytes 688136 | tf_op jit(solution)/shard_map/ppermute | solution.py:914
  244.3 20.5 %collective-permute-start.31 = (bf16[576,512]{1,0:T(8,128)(2,1)}, bf16[576,512]{1,0:T(8,128)(2,1)S(1)}, u32[]{:S(2)}, u32[]{:S(2)}) collective-permute-start(bf16[576,512]{1,0:T(8,128)(2,1)} %get-tuple-element.165.refs_23_), channel_id=1, source_target_pairs={{0,6},{1,7},{2,4},{3,5},{4,2},{5,3},{6,0},{7,1},{8,14},{9,15},{10,... | collective-permute-start | bytes 1769480 | tf_op jit(solution)/shard_map/ppermute | solution.py:914
  246.5 29.6 %collective-permute-start.30 = (bf16[576,512]{1,0:T(8,128)(2,1)}, bf16[576,512]{1,0:T(8,128)(2,1)}, u32[]{:S(2)}, u32[]{:S(2)}) collective-permute-start(bf16[576,512]{1,0:T(8,128)(2,1)} %get-tuple-element.166.refs_22_), channel_id=1, source_target_pairs={{0,4},{1,5},{2,6},{3,7},{4,0},{5,1},{6,2},{7,3},{8,12},{9,13},{10,... | collective-permute-start | bytes 1769480 | tf_op jit(solution)/shard_map/ppermute | solution.py:914
  247.6 28.6 %collective-permute-start.29 = (bf16[576,512]{1,0:T(8,128)(2,1)}, bf16[576,512]{1,0:T(8,128)(2,1)}, u32[]{:S(2)}, u32[]{:S(2)}) collective-permute-start(bf16[576,512]{1,0:T(8,128)(2,1)} %get-tuple-element.164.refs_21_), channel_id=1, source_target_pairs={{0,2},{1,3},{2,0},{3,1},{4,6},{5,7},{6,4},{7,5},{8,10},{9,11},{10,... | collective-permute-start | bytes 1769480 | tf_op jit(solution)/shard_map/ppermute | solution.py:914
  297.3 70.0 %all-reduce.6.cloned.1.call-start = ((), (), s32[]{:S(2)}) async-start(), calls=%async_computation.1 | async-start | bytes 1638400 | tf_op jit(solution)/shard_map/psum | solution.py:969
  298.0 23.5 %collective-permute-start.32 = (bf16[576,512]{1,0:T(8,128)(2,1)}, bf16[576,512]{1,0:T(8,128)(2,1)}, u32[]{:S(2)}, u32[]{:S(2)}) collective-permute-start(bf16[576,512]{1,0:T(8,128)(2,1)} %get-tuple-element.158), channel_id=1, source_target_pairs={{0,8},{8,0},{16,24},{24,16},{1,9},{9,1},{17,25},{25,17},{2,10},{10... | collective-permute-start | bytes 1769480 | tf_op jit(solution)/shard_map/ppermute | solution.py:914
  307.5 63.4 %collective-permute-start.23 = (bf16[4,224,512]{2,1,0:T(8,128)(2,1)}, bf16[4,224,512]{2,1,0:T(8,128)(2,1)S(1)}, u32[]{:S(2)}, u32[]{:S(2)}) collective-permute-start(bf16[4,224,512]{2,1,0:T(8,128)(2,1)} %get-tuple-element.119), channel_id=1, source_target_pairs={{0,1},{1,0},{2,3},{3,2},{4,5},{5,4},{6,7},{7,6},{8,9},{9,8},{10,11... | collective-permute-start | bytes 2752520 | tf_op jit(solution)/shard_map/ppermute | solution.py:914
  322.9 61.9 %collective-permute-start.33 = (bf16[576,512]{1,0:T(8,128)(2,1)S(1)}, bf16[576,512]{1,0:T(8,128)(2,1)S(1)}, u32[]{:S(2)}, u32[]{:S(2)}) collective-permute-start(bf16[576,512]{1,0:T(8,128)(2,1)S(1)} %add_convert_fusion.1), channel_id=1, source_target_pairs={{0,16},{8,24},{16,0},{24,8},{1,17},{9,25},{17,1},{25,9},{2,18},{10... | collective-permute-start | bytes 1769480 | tf_op jit(solution)/shard_map/ppermute | solution.py:914
  372.4 12.1 %collective-permute-start.25 = (bf16[224,512]{1,0:T(8,128)(2,1)S(1)}, bf16[224,512]{1,0:T(8,128)(2,1)S(1)}, u32[]{:S(2)}, u32[]{:S(2)}) collective-permute-start(bf16[224,512]{1,0:T(8,128)(2,1)S(1)} %get-tuple-element.172), channel_id=1, source_target_pairs={{0,4},{1,5},{2,6},{3,7},{4,0},{5,1},{6,2},{7,3},{8,12},{9,13},{10,... | collective-permute-start | bytes 688136 | tf_op jit(solution)/shard_map/ppermute | solution.py:914
  373.6 10.9 %collective-permute-start.24 = (bf16[224,512]{1,0:T(8,128)(2,1)S(1)}, bf16[224,512]{1,0:T(8,128)(2,1)S(1)}, u32[]{:S(2)}, u32[]{:S(2)}) collective-permute-start(bf16[224,512]{1,0:T(8,128)(2,1)S(1)} %get-tuple-element.170), channel_id=1, source_target_pairs={{0,2},{1,3},{2,0},{3,1},{4,6},{5,7},{6,4},{7,5},{8,10},{9,11},{10,... | collective-permute-start | bytes 688136 | tf_op jit(solution)/shard_map/ppermute | solution.py:914
  392.4 12.5 %collective-permute-start.28 = (bf16[224,512]{1,0:T(8,128)(2,1)S(1)}, bf16[224,512]{1,0:T(8,128)(2,1)S(1)}, u32[]{:S(2)}, u32[]{:S(2)}) collective-permute-start(bf16[224,512]{1,0:T(8,128)(2,1)S(1)} %add_convert_fusion.13), channel_id=1, source_target_pairs={{0,16},{8,24},{16,0},{24,8},{1,17},{9,25},{17,1},{25,9},{2,18},{10... | collective-permute-start | bytes 688136 | tf_op jit(solution)/shard_map/ppermute | solution.py:914
  (40 other events, 319.1 us)
Sparse Core Ops, SparseCore 0:
  11.3 72.8 all-gather.2
  301.7 65.5 all-reduce.5
